TPU v7x, 512 devices: a whole 4x4x16 slice. The times are simulated.
512 devices in a mesh: ctx: 64 (over z, x), tp: 8 (over y, core).
Axes of the slice: x: 4, y: 4, z: 16, core: 2. Of those that a mesh axis runs over, the one named last changes fastest.
Arguments:
- doc_lengths: int32 [32], replicated, may hold values from 1 to 512, 8192 in all
- ssm_x: bfloat16 [8192, 8192], P('ctx', 'tp'), may hold values from -6 to 6
- ssm_gate: bfloat16 [8192, 8192], P('ctx', 'tp'), may hold values from -6 to 6
- ssm_b: bfloat16 [8192, 2048], P('ctx', 'tp'), may hold values from -6 to 6
- ssm_c: bfloat16 [8192, 2048], P('ctx', 'tp'), may hold values from -0.375 to 0.375
- step_size: float32 [8192, 128], P('ctx', 'tp'), as said below
- decay_rate: float32 [128], P('tp'), as said below
- norm_weight: float32 [8192], P('tp'), may hold values from 0.1 to 1.9
- queries: bfloat16 [8192, 8192], P('ctx', 'tp'), may hold values from -96 to 96
- keys: bfloat16 [8192, 1024], P('ctx', 'tp'), may hold values from -4 to 4
- values: bfloat16 [8192, 1024], P('ctx', 'tp'), may hold values from -6 to 6
Outputs:
- mixed: bfloat16 [8192, 8192], P(('ctx', 'tp'))
- attended: bfloat16 [8192, 8192], P(('ctx', 'tp'))
Inputs may be any that keep to these rules, and one draw needn't show every extreme that they name: `doc_lengths`: every document has at least one token; the longest has exactly 512. `step_size`: Positive. `decay_rate`: Positive, at most 0.04.
All inputs are finite; a program needn't handle non-finite values.
Results may differ from a plain program's by a relative error of at most 0.0049.
Values may be sent and summed in bfloat16 or wider, within the bound.
No kernel may reach another device: no remote copies, remote signals or barrier semaphores. Data moves between devices by JAX's collectives and lax.ppermute only.
A program may use at most 192 MiB of HBM per device.

v0:
```python
import jax
import jax.numpy as jnp
from jax import lax
from jax.sharding import PartitionSpec as P

HEADS = 128
GROUPS = 8
ATT_DIM = 128
DOC_DEVS = 4


NEG_LARGE = -1e30


def prefix(part, axis, combine, identity):
    place = lax.axis_index(axis)
    gathered = jax.tree.map(lambda a: lax.all_gather(a, axis), part)
    state = jax.tree.map(lambda a, e: jnp.zeros_like(a) + jnp.asarray(e, a.dtype), part, identity)

    def one(turn, state):
        return combine(
            state, jax.tree.map(lambda a: lax.dynamic_index_in_dim(a, turn, 0, False), gathered)
        )

    return lax.fori_loop(0, place, one, state)


def passed_along(block, axis, distance):
    devices = range(lax.axis_size(axis))
    route = [(i - distance, i) for i in devices if i - distance in devices]
    return lax.ppermute(block, axis, route)


def doc_starts(doc_lengths):
    return jnp.cumsum(doc_lengths) - doc_lengths


def doc_index(positions, starts):
    return jnp.sum((starts[None, :] <= positions[:, None]).astype(jnp.int32), axis=1) - 1


def block_terms(ssm_x, ssm_b, ssm_c, step_size, decay_rate, doc_ids, prev_id, group_heads):
    tok_rows = ssm_x.shape[0]
    head_count = step_size.shape[1]
    group_count = head_count // group_heads
    head_size = ssm_x.shape[1] // head_count
    state_size = ssm_b.shape[1] // group_count
    inputs = ssm_x.reshape(tok_rows, group_count, group_heads, head_size)
    in_proj = ssm_b.reshape(tok_rows, group_count, state_size)
    out_proj = ssm_c.reshape(tok_rows, group_count, state_size)
    log_decay = -(step_size * decay_rate[None, :])
    cumulative = jnp.cumsum(log_decay, axis=0)
    same_doc = doc_ids[:, None] == doc_ids[None, :]
    causal = jnp.arange(tok_rows)[:, None] >= jnp.arange(tok_rows)[None, :]
    allowed = (same_doc & causal)[None]
    spread = cumulative.T[:, :, None] - cumulative.T[:, None, :]
    weights = (
        jnp.where(allowed, jnp.exp(jnp.where(allowed, spread, 0.0)), 0.0) * step_size.T[:, None, :]
    )
    intersection = jnp.einsum("tgn,sgn->gts", out_proj, in_proj, preferred_element_type=jnp.float32)
    mixing = (
        weights.reshape(group_count, group_heads, tok_rows, tok_rows) * intersection[:, None]
    ).astype(jnp.bfloat16)
    y_intra = jnp.einsum("ghts,sghp->tghp", mixing, inputs, preferred_element_type=jnp.float32)
    final_sum = cumulative[-1]
    tail = (
        jnp.exp(final_sum[None, :] - cumulative)
        * step_size
        * (doc_ids == doc_ids[-1]).astype(jnp.float32)[:, None]
    )
    scaled = (
        inputs.astype(jnp.float32) * tail.reshape(tok_rows, group_count, group_heads)[..., None]
    ).astype(jnp.bfloat16)
    state_local = jnp.einsum("sghp,sgn->ghpn", scaled, in_proj, preferred_element_type=jnp.float32)
    entry = jnp.exp(cumulative) * (doc_ids == prev_id).astype(jnp.float32)[:, None]
    transmit = jnp.exp(final_sum) * (doc_ids[-1] == prev_id).astype(jnp.float32)
    return (y_intra, state_local, entry, transmit.reshape(group_count, group_heads))


def finish_rows(y_intra, entry, carried, ssm_c, ssm_gate, norm_weight):
    tok_rows, group_count, group_heads, head_size = y_intra.shape
    out_proj = ssm_c.reshape(tok_rows, group_count, -1).astype(jnp.float32)
    incoming = jnp.einsum("tgn,ghpn->tghp", out_proj, carried, precision=lax.Precision.HIGHEST)
    mixer_out = y_intra + incoming * entry.reshape(tok_rows, group_count, group_heads)[..., None]
    gate_vals = ssm_gate.reshape(tok_rows, group_count, group_heads, head_size).astype(jnp.float32)
    gated = (mixer_out * jax.nn.silu(gate_vals)).reshape(
        tok_rows, group_count, group_heads * head_size
    )
    factor = lax.rsqrt(jnp.mean(gated * gated, axis=2, keepdims=True) + 1e-05)
    return ((gated * factor).reshape(tok_rows, -1) * norm_weight[None, :]).astype(jnp.bfloat16)


def chain_states(earlier, later):
    return (earlier[0] * later[0], later[0][:, :, None, None] * earlier[1] + later[1])


def attention_update(
    carry, query_rows, key_block, value_block, key_pos, query_pos, query_doc, starts
):
    running_max, running_sum, running_acc = carry
    block_rows = key_block.shape[0]
    kv_local = key_block.shape[1] // ATT_DIM
    key_heads = key_block.reshape(block_rows, kv_local, ATT_DIM)
    value_heads = value_block.reshape(block_rows, kv_local, ATT_DIM)
    key_doc = doc_index(key_pos, starts)
    allowed = (query_doc[:, None] == key_doc[None, :]) & (key_pos[None, :] <= query_pos[:, None])
    scores = jnp.einsum(
        "tngd,knd->ngtk", query_rows, key_heads, preferred_element_type=jnp.float32
    ) * ATT_DIM ** (-0.5)
    scores = jnp.where(allowed[None, None], scores, -jnp.inf)
    new_max = jnp.maximum(running_max, jnp.max(scores, axis=3))
    probs = jnp.exp(scores - new_max[..., None])
    factor = jnp.exp(running_max - new_max)
    new_sum = running_sum * factor + jnp.sum(probs, axis=3)
    weighted = jnp.einsum(
        "ngtk,knd->ngtd",
        probs.astype(jnp.bfloat16),
        value_heads,
        preferred_element_type=jnp.float32,
    )
    return (new_max, new_sum, running_acc * factor[..., None] + weighted)


def local(
    doc_lengths,
    ssm_x,
    ssm_gate,
    ssm_b,
    ssm_c,
    step_size,
    decay_rate,
    norm_weight,
    queries,
    keys,
    values,
):
    tok_rows = ssm_x.shape[0]
    ctx_index = lax.axis_index("ctx")
    begin = ctx_index * tok_rows
    positions = begin + jnp.arange(tok_rows, dtype=jnp.int32)
    starts = doc_starts(doc_lengths)
    doc_ids = doc_index(positions, starts)
    prev_id = doc_index(jnp.reshape(begin - 1, (1,)), starts)[0]
    group_heads = HEADS // GROUPS
    y_intra, state_local, entry, transmit = block_terms(
        ssm_x, ssm_b, ssm_c, step_size, decay_rate, doc_ids, prev_id, group_heads
    )
    scanned = prefix(
        (transmit, state_local),
        "ctx",
        chain_states,
        (jnp.ones_like(transmit), jnp.zeros_like(state_local)),
    )
    carried = scanned[1]
    mixed_rows = finish_rows(y_intra, entry, carried, ssm_c, ssm_gate, norm_weight)
    kv_local = keys.shape[1] // ATT_DIM
    q_groups = queries.shape[1] // (kv_local * ATT_DIM)
    query_rows = queries.reshape(tok_rows, kv_local, q_groups, ATT_DIM)
    floor_start = jnp.max(jnp.where(starts <= begin, starts, 0))
    query_last = begin + tok_rows - 1
    carry_shape = (kv_local, q_groups, tok_rows)
    initial = (
        jnp.full(carry_shape, NEG_LARGE, jnp.float32),
        jnp.zeros(carry_shape, jnp.float32),
        jnp.zeros(carry_shape + (ATT_DIM,), jnp.float32),
    )

    def visit(carry, key_block, value_block, key_begin):
        block_rows = key_block.shape[0]
        needed = (key_begin <= query_last) & (key_begin + block_rows - 1 >= floor_start)

        def update(inner):
            key_pos = key_begin + jnp.arange(block_rows, dtype=jnp.int32)
            return attention_update(
                inner, query_rows, key_block, value_block, key_pos, positions, doc_ids, starts
            )

        def unchanged(inner):
            return inner

        return lax.cond(needed, update, unchanged, carry)

    totals = visit(initial, keys, values, begin)
    for hop_count in range(1, DOC_DEVS + 1):
        near_keys, near_values = passed_along((keys, values), "ctx", hop_count)
        totals = visit(totals, near_keys, near_values, begin - hop_count * tok_rows)
    final_out = totals[2] / totals[1][..., None]
    attended_rows = (
        jnp.transpose(final_out, (2, 0, 1, 3)).reshape(tok_rows, -1).astype(jnp.bfloat16)
    )
    mixed_local, attended_local = (
        lax.all_to_all(mixed_rows, "tp", split_axis=0, concat_axis=1, tiled=True),
        lax.all_to_all(attended_rows, "tp", split_axis=0, concat_axis=1, tiled=True),
    )
    return (mixed_local, attended_local)


def solution(mesh):
    return jax.shard_map(
        local,
        mesh=mesh,
        in_specs=(
            P(),
            P("ctx", "tp"),
            P("ctx", "tp"),
            P("ctx", "tp"),
            P("ctx", "tp"),
            P("ctx", "tp"),
            P("tp"),
            P("tp"),
            P("ctx", "tp"),
            P("ctx", "tp"),
            P("ctx", "tp"),
        ),
        out_specs=(P(("ctx", "tp"), None), P(("ctx", "tp"), None)),
        check_vma=False,
    )
```

profile of v0, /device:TPU:486, one launch (start us, length us, event | category | flops | bytes accessed | tf_op | source)
XLA Modules:
  0.0 647.3 jit_solution(1013280911103433787)
XLA Ops:
  35.4 2.4 conditional.5
  37.8 87.7 %all-gather.2 = f32[64,1,16]{2,1,0:T(1,128)S(1)} all-gather(f32[1,1,16]{2,1,0:T(1,128)S(1)} %get-tuple-element.489), channel_id=2, replica_groups=mesh['ctx'=64,'tp'=8] {'ctx'}, dimensions={0}, use_global_device_ids=true | all-gather | bytes 4160 | tf_op jit(solution)/shard_map/all_gather | solution.py:17
  129.9 4.5 all-to-all-start.1
  134.4 393.3 %all-gather.5.cloned.1.call-done = f32[1024,64,256]{2,1,0:T(8,128)} async-done(((f32[16,64,256]{2,1,0:T(8,128)}), f32[1024,64,256]{2,1,0:T(8,128)}) %all-gather.5.cloned.1.call-update) | async-done | bytes 67108880 | tf_op jit(solution)/shard_map/all_gather | solution.py:17
  527.8 96.1 %while.12 = (s32[]{:T(128)}, f32[1,16,64,256]{3,2,1,0:T(8,128)S(1)}, s32[]{:T(128)}, f32[64,1,16]{2,1,0:T(1,128)S(1)}, f32[64,1,16,64,256]{4,3,2,1,0:T(8,128)}, /*index=5*/s32[]{:T(128)}, s32[]{:T(128)}, s32[]{:T(128)}) while((s32[]{:T(128)}, f32[1,16,64,256]{3,2,1,0:T(8,128)S(1)}, s32[]{:T(128)}, f32[64,1,16]{2,1,0:T(1,128)S(1)}, ...), condition=%wide.region_5.6_spmd, body=%wide.region_4.5_spmd.sunk | while | flops 524293 | bytes 3146047 | solution.py:25
  527.9 1.5 bitcast_add_fusion.7
  529.4 1.5 bitcast_add_fusion.7
  530.9 1.5 bitcast_add_fusion.7
  532.4 1.5 bitcast_add_fusion.7
  534.0 1.5 bitcast_add_fusion.7
  535.5 1.5 bitcast_add_fusion.7
  537.0 1.5 bitcast_add_fusion.7
  538.6 1.5 bitcast_add_fusion.7
  540.1 1.5 bitcast_add_fusion.7
  541.6 1.5 bitcast_add_fusion.7
  543.1 1.5 bitcast_add_fusion.7
  544.7 1.5 bitcast_add_fusion.7
  546.2 1.5 bitcast_add_fusion.7
  547.7 1.5 bitcast_add_fusion.7
  549.2 1.5 bitcast_add_fusion.7
  550.8 1.5 bitcast_add_fusion.7
  552.3 1.5 bitcast_add_fusion.7
  553.8 1.5 bitcast_add_fusion.7
  555.3 1.5 bitcast_add_fusion.7
  556.9 1.5 bitcast_add_fusion.7
  558.4 1.5 bitcast_add_fusion.7
  582.8 1.5 bitcast_add_fusion.7
  611.8 1.5 bitcast_add_fusion.7
  624.0 1.5 multiply_reduce_fusion
  626.4 1.5 multiply_convert_fusion.2
  627.9 4.3 all-to-all-start
  632.9 6.8 %all-to-all-done = bf16[8,16,1024]{2,1,0:T(8,128)(2,1)S(1)} async-done(((bf16[8,16,1024]{2,1,0:T(8,128)(2,1)}), bf16[8,16,1024]{2,1,0:T(8,128)(2,1)S(1)}, u32[]{:S(2)}, u32[]{:S(2)}) %all-to-all-start) | async-done | bytes 262176 | tf_op jit(solution)/shard_map/all_to_all | solution.py:192
  (203 shorter events, 95.0 us)
Async XLA Ops:
  7.2 8.1 %copy-start = (bf16[128,256]{1,0:T(8,128)(2,1)S(1)}, bf16[128,256]{1,0:T(8,128)(2,1)}, u32[]{:S(2)}) copy-start(bf16[128,256]{1,0:T(8,128)(2,1)} %param.26) | copy-start | bytes 196612
  7.2 520.6 %all-gather.5.cloned.1.call-start = ((), (), s32[]{:S(2)}) async-start(), calls=%async_computation.2 | async-start | bytes 68157440 | tf_op jit(solution)/shard_map/all_gather | solution.py:17
  16.5 7.7 %collective-permute-start = (bf16[128,128]{1,0:T(8,128)(2,1)}, bf16[128,128]{1,0:T(8,128)(2,1)S(1)}, u32[]{:S(2)}, u32[]{:S(2)}) collective-permute-start(bf16[128,128]{1,0:T(8,128)(2,1)} %param.32), channel_id=1, source_target_pairs={{0,8},{8,16},{16,24},{24,32},{32,40},{40,48},{48,56},{56,64},{64,7... | collective-permute-start | bytes 98312 | tf_op jit(solution)/shard_map/ppermute | solution.py:31
  17.8 9.2 %collective-permute-start.2 = (bf16[128,128]{1,0:T(8,128)(2,1)}, bf16[128,128]{1,0:T(8,128)(2,1)S(1)}, u32[]{:S(2)}, u32[]{:S(2)}) collective-permute-start(bf16[128,128]{1,0:T(8,128)(2,1)} %param.32), channel_id=1, source_target_pairs={{0,16},{8,24},{16,32},{24,40},{32,48},{40,56},{48,64},{56,72},{64,... | collective-permute-start | bytes 98312 | tf_op jit(solution)/shard_map/ppermute | solution.py:31
  19.1 6.7 %collective-permute-start.1 = (bf16[128,128]{1,0:T(8,128)(2,1)}, bf16[128,128]{1,0:T(8,128)(2,1)S(1)}, u32[]{:S(2)}, u32[]{:S(2)}) collective-permute-start(bf16[128,128]{1,0:T(8,128)(2,1)} %param.33), channel_id=1, source_target_pairs={{0,8},{8,16},{16,24},{24,32},{32,40},{40,48},{48,56},{56,64},{64,7... | collective-permute-start | bytes 98312 | tf_op jit(solution)/shard_map/ppermute | solution.py:31
  20.4 106.1 %collective-permute-start.3 = (bf16[128,128]{1,0:T(8,128)(2,1)}, bf16[128,128]{1,0:T(8,128)(2,1)S(1)}, u32[]{:S(2)}, u32[]{:S(2)}) collective-permute-start(bf16[128,128]{1,0:T(8,128)(2,1)} %param.33), channel_id=1, source_target_pairs={{0,16},{8,24},{16,32},{24,40},{32,48},{40,56},{48,64},{56,72},{64,... | collective-permute-start | bytes 98312 | tf_op jit(solution)/shard_map/ppermute | solution.py:31
  21.7 105.9 %collective-permute-start.4 = (bf16[128,128]{1,0:T(8,128)(2,1)}, bf16[128,128]{1,0:T(8,128)(2,1)S(1)}, u32[]{:S(2)}, u32[]{:S(2)}) collective-permute-start(bf16[128,128]{1,0:T(8,128)(2,1)} %param.32), channel_id=1, source_target_pairs={{0,24},{8,32},{16,40},{24,48},{32,56},{40,64},{48,72},{56,80},{64,... | collective-permute-start | bytes 98312 | tf_op jit(solution)/shard_map/ppermute | solution.py:31
  24.2 103.4 %collective-permute-start.5 = (bf16[128,128]{1,0:T(8,128)(2,1)}, bf16[128,128]{1,0:T(8,128)(2,1)S(1)}, u32[]{:S(2)}, u32[]{:S(2)}) collective-permute-start(bf16[128,128]{1,0:T(8,128)(2,1)} %param.33), channel_id=1, source_target_pairs={{0,24},{8,32},{16,40},{24,48},{32,56},{40,64},{48,72},{56,80},{64,... | collective-permute-start | bytes 98312 | tf_op jit(solution)/shard_map/ppermute | solution.py:31
  25.8 102.9 %collective-permute-start.6 = (bf16[128,128]{1,0:T(8,128)(2,1)}, bf16[128,128]{1,0:T(8,128)(2,1)S(1)}, u32[]{:S(2)}, u32[]{:S(2)}) collective-permute-start(bf16[128,128]{1,0:T(8,128)(2,1)} %param.32), channel_id=1, source_target_pairs={{0,32},{8,40},{16,48},{24,56},{32,64},{40,72},{48,80},{56,88},{64,... | collective-permute-start | bytes 98312 | tf_op jit(solution)/shard_map/ppermute | solution.py:31
  27.1 101.6 %collective-permute-start.7 = (bf16[128,128]{1,0:T(8,128)(2,1)}, bf16[128,128]{1,0:T(8,128)(2,1)S(1)}, u32[]{:S(2)}, u32[]{:S(2)}) collective-permute-start(bf16[128,128]{1,0:T(8,128)(2,1)} %param.33), channel_id=1, source_target_pairs={{0,32},{8,40},{16,48},{24,56},{32,64},{40,72},{48,80},{56,88},{64,... | collective-permute-start | bytes 98312 | tf_op jit(solution)/shard_map/ppermute | solution.py:31
  129.9 497.9 %all-to-all-start.1 = ((bf16[8,16,1024]{2,1,0:T(8,128)(2,1)}), bf16[8,16,1024]{2,1,0:T(8,128)(2,1)S(1)}, u32[]{:S(2)}, u32[]{:S(2)}) async-start(bf16[8,16,1024]{2,1,0:T(8,128)(2,1)} %convert_element_type.139), calls=%async_computation.1 | async-start | bytes 524288 | tf_op jit(solution)/shard_map/all_to_all | solution.py:193
  627.9 11.8 %all-to-all-start = ((bf16[8,16,1024]{2,1,0:T(8,128)(2,1)}), bf16[8,16,1024]{2,1,0:T(8,128)(2,1)S(1)}, u32[]{:S(2)}, u32[]{:S(2)}) async-start(bf16[8,16,1024]{2,1,0:T(8,128)(2,1)} %multiply_convert_fusion.2), calls=%async_computation | async-start | bytes 524288 | tf_op jit(solution)/shard_map/all_to_all | solution.py:192
Sparse Core Ops, SparseCore 0:
  16.7 511.0 all-gather.4
where the time goes:
time: 651 us; the launch traced here: 647 us
  waiting for transfers between devices  400 us (61%)
  other arithmetic  99.6 us (15%)
  blocking collectives  87.7 us (13%)
  starting transfers between devices  19.1 us (3%)
  between operations  19 us (3%)
  local copies, waits for them, and re-layouts  9.62 us (1%)
  matrix products  8.96 us (1%)
    all_gather x1, waiting for transfers between devices, prefix(): gathered = jax.tree.map(lambda a: lax.all_gather(a, axis), part)  393 us
    add x63, other arithmetic, chain_states(): later[0][:, :, None, None] * earlier[1] + later[1]  93.1 us
    all_gather x1, blocking collectives, prefix(): gathered = jax.tree.map(lambda a: lax.all_gather(a, axis), part)  87.7 us
  transfers between devices with their start and end apart: 11, of which 3 were waited for; matrix products, arithmetic and copies ran while one was open for 17% of the time, Pallas kernels for 0%

commit v1 on v0

v1 whole, which is shorter than its diff:
```python
import functools

import jax
import jax.numpy as jnp
from jax import lax
from jax.experimental import pallas as pl
from jax.experimental.pallas import tpu as pltpu
from jax.sharding import Mesh, PartitionSpec as P

ROWS = 128
HALF = 64
GROUP_HEADS = 16
Q_HEADS = 8
PEERS = 4
STATE = 256
SCALE = 128**-0.5
NEG = -1e30
F32 = jnp.float32
BF16 = jnp.bfloat16
VMEM = pl.BlockSpec(memory_space=pltpu.VMEM)
SMEM = pl.BlockSpec(memory_space=pltpu.SMEM)


def call(kernel, outs, specs, flops=0, moved=0, exps=0):
    return pl.pallas_call(
        kernel,
        out_shape=outs,
        in_specs=specs,
        out_specs=jax.tree.map(lambda _: VMEM, outs),
        compiler_params=pltpu.CompilerParams(vmem_limit_bytes=32 * 2**20),
        cost_estimate=pl.CostEstimate(flops=flops, bytes_accessed=moved, transcendentals=exps),
    )


def shaped(shape, dtype):
    return jax.ShapeDtypeStruct(shape, dtype)


def dot(a, b, dims=((1,), (0,)), precision=None):
    return lax.dot_general(
        a, b, (dims, ((), ())), precision=precision, preferred_element_type=F32
    )


def three_parts(a):
    high = a.astype(BF16)
    rest = a - high.astype(F32)
    middle = rest.astype(BF16)
    low = (rest - middle.astype(F32)).astype(BF16)
    return high, middle, low


def start_row(doc_ref, begin):
    pos = begin + lax.broadcasted_iota(jnp.int32, (8, ROWS), 1)
    found = jnp.zeros((8, ROWS), jnp.int32)
    last = jnp.int32(0)
    start = jnp.int32(0)
    for j in range(doc_ref.shape[0]):
        found = jnp.where(pos >= start, start, found)
        last = jnp.where(begin + ROWS - 1 >= start, start, last)
        start = start + doc_ref[j]
    return found, last


def head_rows(dt_ref, rate_ref):
    row = lax.broadcasted_iota(jnp.int32, (GROUP_HEADS, ROWS), 0)
    rate = jnp.zeros((GROUP_HEADS, ROWS), F32)
    for h in range(GROUP_HEADS):
        rate = jnp.where(row == h, rate_ref[h], rate)
    dt = dt_ref[...]
    upto = lax.broadcasted_iota(jnp.int32, (ROWS, ROWS), 0) <= lax.broadcasted_iota(
        jnp.int32, (ROWS, ROWS), 1
    )
    decay = -(dt * rate)
    upto = upto.astype(F32).astype(BF16)
    total = sum(dot(part, upto) for part in three_parts(decay))
    return dt, total


def spread_heads(parts):
    width = GROUP_HEADS * HALF
    lane = lax.broadcasted_iota(jnp.int32, (GROUP_HEADS, width), 1)
    row = lax.broadcasted_iota(jnp.int32, (GROUP_HEADS, width), 0)
    pick = ((lane >= row * HALF) & (lane < (row + 1) * HALF)).astype(F32).astype(BF16)
    return sum(dot(part, pick, ((0,), (0,))) for part in parts)


def prepare(doc_ref, begin_ref, rate_ref, x_ref, b_ref, dt_ref, k_ref, v_ref, out_ref, kv_ref):
    begin = begin_ref[0]
    _, last_start = start_row(doc_ref, begin)
    dt, total = head_rows(dt_ref, rate_ref)
    final = total[:, ROWS - 1 :]
    pos = begin + lax.broadcasted_iota(jnp.int32, (GROUP_HEADS, ROWS), 1)
    tail = jnp.where(pos >= last_start, jnp.exp(final - total) * dt, 0.0)
    tail = spread_heads(three_parts(tail))
    scaled = (x_ref[...].astype(F32) * tail).astype(BF16)
    whole = jnp.broadcast_to(final, (GROUP_HEADS, ROWS))
    transmit = jnp.where(last_start < begin, jnp.exp(whole), 0.0)
    parts = three_parts(spread_heads([p[:, :16] for p in three_parts(transmit)]))
    row = lax.broadcasted_iota(jnp.int32, (16, GROUP_HEADS * HALF), 0)
    sent = jnp.where(
        row == 0,
        parts[0].astype(F32),
        jnp.where(row == 1, parts[1].astype(F32), parts[2].astype(F32)),
    ).astype(BF16)
    state = dot(b_ref[...], scaled, ((0,), (0,))).astype(BF16)
    width = GROUP_HEADS * HALF // PEERS
    for j in range(PEERS):
        out_ref[j, :STATE, :] = state[:, j * width : (j + 1) * width]
        out_ref[j, STATE:, :] = sent[:, j * width : (j + 1) * width]
    kv_ref[:, :ROWS] = k_ref[...]
    kv_ref[:, ROWS:] = v_ref[...]


def received(ref, j):
    state = ref[j, :STATE, :].astype(F32)
    parts = ref[j, STATE:, :].astype(F32)
    return state, parts[0:1] + parts[1:2] + parts[2:3]


def group_state(got_ref, kv_ref, out_ref):
    total, _ = received(got_ref, 0)
    for j in range(1, PEERS):
        state, transmit = received(got_ref, j)
        total = total * transmit + state
    out_ref[:STATE, :] = total.astype(BF16)
    out_ref[STATE:, :] = kv_ref[...]


def carried_states(got_ref, before_ref, out_ref):
    carried = before_ref[:STATE, :].astype(F32)
    for j in range(PEERS):
        out_ref[j] = carried.astype(BF16)
        if j < PEERS - 1:
            state, transmit = received(got_ref, j)
            carried = carried * transmit + state


def start_columns(doc_ref, begin):
    found, _ = start_row(doc_ref, begin)
    return jnp.transpose(jnp.broadcast_to(found[:1].astype(F32), (ROWS, ROWS)))


def inside(doc_ref, begin_ref, rate_ref, x_ref, b_ref, c_ref, dt_ref, gate_ref, own_ref, factor_ref):
    begin = begin_ref[0]
    starts = start_columns(doc_ref, begin)
    row = lax.broadcasted_iota(jnp.int32, (ROWS, ROWS), 0)
    lane = lax.broadcasted_iota(jnp.int32, (ROWS, ROWS), 1)
    allowed = (lane <= row) & ((begin + lane).astype(F32) >= starts)
    continued = starts < begin.astype(F32)
    dt, total = head_rows(dt_ref, rate_ref)
    tall = jnp.transpose(jnp.concatenate([total, jnp.zeros((ROWS - GROUP_HEADS, ROWS), F32)], 0))
    inner = dot(c_ref[...], b_ref[...], ((1,), (1,)))
    left = lane < HALF
    for pair in range(GROUP_HEADS // 2):
        at = slice(pair * ROWS, (pair + 1) * ROWS)
        columns, mixing = [], []
        for h in (2 * pair, 2 * pair + 1):
            column = jnp.broadcast_to(tall[:, h : h + 1], (ROWS, ROWS))
            spread = jnp.where(allowed, column - total[h : h + 1], NEG)
            mixing.append((jnp.exp(spread) * dt[h : h + 1] * inner).astype(BF16))
            columns.append(column)
        x = x_ref[:, at]
        zero = jnp.zeros_like(x)
        blocks = jnp.concatenate([jnp.where(left, x, zero), jnp.where(left, zero, x)], 0)
        own = dot(jnp.concatenate(mixing, 1), blocks)
        entry = jnp.where(continued, jnp.exp(jnp.where(left, columns[0], columns[1])), 0.0)
        gate = gate_ref[:, at].astype(F32)
        gate = gate / (1.0 + jnp.exp(-gate))
        own_ref[:, at] = own * gate
        factor_ref[:, at] = entry * gate


def attention(doc_ref, begin_ref, q_ref, kv0_ref, kv1_ref, kv2_ref, kv3_ref, kv4_ref, out_ref):
    begin = begin_ref[0]
    starts = start_columns(doc_ref, begin)
    row = lax.broadcasted_iota(jnp.int32, (ROWS, ROWS), 0)
    lane = lax.broadcasted_iota(jnp.int32, (ROWS, ROWS), 1)
    blocks = [kv0_ref[...], kv1_ref[...], kv2_ref[...], kv3_ref[...], kv4_ref[STATE:, :]]
    bias = []
    for j in range(len(blocks)):
        allowed = (begin - j * ROWS + lane).astype(F32) >= starts
        if j == 0:
            allowed = allowed & (lane <= row)
        bias.append(jnp.where(allowed, 0.0, NEG))
    bias = jnp.concatenate(bias, 1)
    keys = jnp.concatenate([b[:, :ROWS] for b in blocks], 0)
    values = jnp.concatenate([b[:, ROWS:] for b in blocks], 0)
    for h in range(Q_HEADS):
        at = slice(h * ROWS, (h + 1) * ROWS)
        scores = dot(q_ref[:, at], keys, ((1,), (1,))) * SCALE + bias
        top = jnp.max(scores, axis=1, keepdims=True)
        probs = jnp.exp(scores - top)
        total = jnp.sum(probs, axis=1, keepdims=True)
        out_ref[:, at] = (dot(probs.astype(BF16), values) / total).astype(BF16)


def finish(c_ref, carried_ref, own_ref, factor_ref, weight_ref, att_ref, out_ref, scratch_ref):
    width = GROUP_HEADS * HALF // PEERS
    squares = jnp.zeros((ROWS, 1), F32)
    c = c_ref[...]
    for j in range(PEERS):
        at = slice(j * width, (j + 1) * width)
        gated = own_ref[:, at] + factor_ref[:, at] * dot(c, carried_ref[j])
        scratch_ref[:, at] = gated
        squares = squares + jnp.sum(gated * gated, axis=1, keepdims=True)
    scale = lax.rsqrt(squares * (1.0 / (GROUP_HEADS * HALF)) + 1e-05)
    for j in range(PEERS):
        at = slice(j * width, (j + 1) * width)
        out_ref[:, at] = (scratch_ref[:, at] * scale * weight_ref[:, at]).astype(BF16)
    out_ref[:, GROUP_HEADS * HALF :] = att_ref[...]


def lay_out(got_ref, mixed_ref, attended_ref):
    width = GROUP_HEADS * HALF
    for j in range(got_ref.shape[0]):
        mixed_ref[:, j * width : (j + 1) * width] = got_ref[j, :, :width]
        attended_ref[:, j * width : (j + 1) * width] = got_ref[j, :, width:]


def local(doc, x, gate, b, c, dt, rate, weight, q, k, v):
    width = GROUP_HEADS * HALF
    tp = lax.axis_size("tp")
    block = lax.axis_index("z") * PEERS + lax.axis_index("x")
    begin = jnp.reshape(block * ROWS, (1,)).astype(jnp.int32)
    dt = dt.T
    own_states, kv = call(
        prepare,
        (shaped((PEERS, STATE + 16, width // PEERS), BF16), shaped((ROWS, 2 * ROWS), BF16)),
        [SMEM, SMEM, SMEM] + [VMEM] * 5,
        flops=10**8,
        moved=10**6,
    )(doc, begin, rate, x, b, dt, k, v)
    got = lax.all_to_all(own_states, "x", 0, 0, tiled=True)

    def along(a, distance):
        count = lax.axis_size("z") * PEERS
        return lax.ppermute(a, ("z", "x"), [(i - distance, i) for i in range(distance, count)])

    near = [along(kv, d) for d in range(1, PEERS)]
    group = call(
        group_state,
        shaped((STATE + ROWS, width // PEERS), BF16),
        [VMEM] * 2,
        flops=10**6,
        moved=10**6,
    )(got, kv)
    before = lax.ppermute(group, "z", [(i - 1, i) for i in range(1, lax.axis_size("z"))])
    carried = call(
        carried_states,
        shaped((PEERS, STATE, width // PEERS), BF16),
        [VMEM] * 2,
        flops=10**6,
        moved=10**6,
    )(got, before)
    carried = lax.all_to_all(carried, "x", 0, 0, tiled=True)
    own, factor = call(
        inside,
        (shaped((ROWS, width), F32), shaped((ROWS, width), F32)),
        [SMEM, SMEM, SMEM] + [VMEM] * 5,
        flops=10**8,
        moved=10**6,
        exps=400000,
    )(doc, begin, rate, x, b, c, dt, gate)
    att = call(
        attention,
        shaped((ROWS, width), BF16),
        [SMEM, SMEM] + [VMEM] * 6,
        flops=4 * 10**8,
        moved=10**6,
        exps=700000,
    )(doc, begin, q, kv, *near, before)
    rows = pl.pallas_call(
        finish,
        out_shape=shaped((ROWS, 2 * width), BF16),
        in_specs=[VMEM] * 6,
        out_specs=VMEM,
        scratch_shapes=[pltpu.VMEM((ROWS, width), F32)],
        compiler_params=pltpu.CompilerParams(vmem_limit_bytes=32 * 2**20),
        cost_estimate=pl.CostEstimate(flops=10**8, bytes_accessed=10**6, transcendentals=128),
    )(c, carried, own, factor, weight.reshape(1, width), att)
    moved = lax.all_to_all(rows.reshape(tp, ROWS // tp, 2 * width), "tp", 0, 0, tiled=True)
    return call(
        lay_out,
        (shaped((ROWS // tp, tp * width), BF16), shaped((ROWS // tp, tp * width), BF16)),
        [VMEM],
        moved=10**6,
    )(moved)


def solution(mesh):
    sizes = dict(mesh.shape)
    inner = Mesh(
        mesh.devices.reshape(sizes["ctx"] // PEERS, PEERS, sizes["tp"]), ("z", "x", "tp")
    )
    both = P(("z", "x"), "tp")
    return jax.shard_map(
        local,
        mesh=inner,
        in_specs=(P(), both, both, both, both, both, P("tp"), P("tp"), both, both, both),
        out_specs=(P(("z", "x", "tp"), None), P(("z", "x", "tp"), None)),
        check_vma=False,
    )
```

time: 651 us -> 72.7 us (0.11)
  the two profiles are of different devices: /device:TPU:486 before, /device:TPU:224 now
where the time goes in v1:
time: 72.7 us; the launch traced here: 72.1 us
  blocking collectives  28.6 us (39%)
  starting transfers between devices  22.5 us (31%)
  Pallas kernels  8.33 us (11%)
  waiting for transfers between devices  7.17 us (10%)
  local copies, waits for them, and re-layouts  4.67 us (6%)
  between operations  0.81 us (1%)
    all_to_all x1, blocking collectives, local(): lax.all_to_all(rows.reshape(tp, ROWS // tp, 2 * width), 'tp', 0, 0, tiled...  14.7 us
    all_to_all x1, blocking collectives, local(): got = lax.all_to_all(own_states, 'x', 0, 0, tiled=True)  13.9 us
    ppermute x3, starting transfers between devices, along(): lax.ppermute(a, ('z', 'x'), [(i - distance, i) for i in range(distance, c...  13.9 us
    ppermute x1, starting transfers between devices, local(): lax.ppermute(group, 'z', [(i - 1, i) for i in range(1, lax.axis_size('z'))])  5.04 us
    unnamed x26, local copies, waits for them, and re-layouts  4.67 us
    ppermute x3, waiting for transfers between devices, along(): lax.ppermute(a, ('z', 'x'), [(i - distance, i) for i in range(distance, c...  4 us
    all_to_all x1, starting transfers between devices, local(): carried = lax.all_to_all(carried, 'x', 0, 0, tiled=True)  3.61 us
    ppermute x1, waiting for transfers between devices, local(): lax.ppermute(group, 'z', [(i - 1, i) for i in range(1, lax.axis_size('z'))])  3.17 us
  transfers between devices with their start and end apart: 5, of which 2 were waited for; matrix products, arithmetic and copies ran while one was open for 0% of the time, Pallas kernels for 6%

profile of v1, /device:TPU:224, one launch (start us, length us, event | category | flops | bytes accessed | tf_op | source)
XLA Modules:
  0.0 72.1 jit_solution(5809509037397467227)
XLA Ops:
  0.6 0.0 copy-start.7
  0.6 0.0 copy-start.9
  0.7 0.0 copy-start.10
  0.7 0.7 copy-done.7
  1.3 0.0 copy-done.9
  1.3 0.0 copy-done.10
  1.3 0.9 %copy-done = bf16[128,1024]{1,0:T(8,128)(2,1)S(1)} copy-done((bf16[128,1024]{1,0:T(8,128)(2,1)S(1)}, bf16[128,1024]{1,0:T(8,128)(2,1)}, u32[]{:S(2)}) %copy-start) | copy-done | bytes 262168
  2.3 0.8 %copy-done.2 = bf16[128,256]{1,0:T(8,128)(2,1)S(1)} copy-done((bf16[128,256]{1,0:T(8,128)(2,1)S(1)}, bf16[128,256]{1,0:T(8,128)(2,1)}, u32[]{:S(2)}) %copy-start.2) | copy-done | bytes 65560
  3.1 0.8 %copy-done.5 = bf16[128,128]{1,0:T(8,128)(2,1)S(1)} copy-done((bf16[128,128]{1,0:T(8,128)(2,1)S(1)}, bf16[128,128]{1,0:T(8,128)(2,1)}, u32[]{:S(2)}) %copy-start.5) | copy-done | bytes 32792
  3.9 0.8 %copy-done.6 = bf16[128,128]{1,0:T(8,128)(2,1)S(1)} copy-done((bf16[128,128]{1,0:T(8,128)(2,1)S(1)}, bf16[128,128]{1,0:T(8,128)(2,1)}, u32[]{:S(2)}) %copy-start.6) | copy-done | bytes 32792
  4.6 1.6 %shard_map.122 = (bf16[4,272,256]{2,1,0:T(8,128)(2,1)S(1)}, bf16[128,256]{1,0:T(8,128)(2,1)S(1)}) custom-call(s32[32]{0:T(128)S(1)} %copy-done.10, s32[1]{0:T(128)} %bitcast.begin_ref, f32[16]{0:T(128)S(1)} %copy-done.9, bf16[128,1024]{1,0:T(8,128)(2,1)S(1)} %copy-done, bf16[128,256]{1,0:T(8,128)(2,1)S(1)} %copy-done.2, f32[16,128]{1,0:T(8,128)S(1)} %bitcast.5, ...), custom_call_target="tpu_custom_call" | custom-call | flops 100000000 | bytes 1000000 | tf_op jit(solution)/shard_map/pallas_call | solution.py:227
  6.2 13.9 %all_to_all.15.got_ref = bf16[4,272,256]{2,1,0:T(8,128)(2,1)S(1)} all-to-all(bf16[4,272,256]{2,1,0:T(8,128)(2,1)S(1)} %get-tuple-element.6), channel_id=1, replica_groups=mesh['z'=16,'x'=4,'tp'=8] {'x'}, dimensions={0} | all-to-all | bytes 1114112 | tf_op jit(solution)/shard_map/all_to_all | solution.py:234
  20.1 0.1 shard_map.123
  20.2 5.0 %collective-permute-start = (bf16[384,256]{1,0:T(8,128)(2,1)S(1)}, bf16[384,256]{1,0:T(8,128)(2,1)S(1)}, u32[]{:S(2)}, u32[]{:S(2)}) collective-permute-start(bf16[384,256]{1,0:T(8,128)(2,1)S(1)} %shard_map.123), channel_id=1, source_target_pairs={{0,32},{32,64},{64,96},{96,128},{128,160},{160,192},{192,224},{224... | collective-permute-start | bytes 589832 | tf_op jit(solution)/shard_map/ppermute | solution.py:248
  25.3 3.2 %collective-permute-done.before_ref.kv4_ref = bf16[384,256]{1,0:T(8,128)(2,1)S(1)} collective-permute-done((bf16[384,256]{1,0:T(8,128)(2,1)S(1)}, bf16[384,256]{1,0:T(8,128)(2,1)S(1)}, u32[]{:S(2)}, u32[]{:S(2)}) %collective-permute-start) | collective-permute-done | bytes 196640 | tf_op jit(solution)/shard_map/ppermute | solution.py:248
  28.4 0.9 %shard_map.124 = bf16[4,256,256]{2,1,0:T(8,128)(2,1)} custom-call(bf16[4,272,256]{2,1,0:T(8,128)(2,1)S(1)} %all_to_all.15.got_ref, bf16[384,256]{1,0:T(8,128)(2,1)S(1)} %collective-permute-done.before_ref.kv4_ref), custom_call_target="tpu_custom_call" | custom-call | flops 1000000 | bytes 1000000 | tf_op jit(solution)/shard_map/pallas_call | solution.py:249
  29.4 3.6 %all-to-all-start.1 = ((bf16[4,256,256]{2,1,0:T(8,128)(2,1)}), bf16[4,256,256]{2,1,0:T(8,128)(2,1)S(1)}, u32[]{:S(2)}, u32[]{:S(2)}) async-start(bf16[4,256,256]{2,1,0:T(8,128)(2,1)} %shard_map.124), calls=%async_computation.1 | async-start | bytes 1048576 | tf_op jit(solution)/shard_map/all_to_all | solution.py:256
  33.0 0.0 copy-start.12
  33.0 5.2 %collective-permute-start.3 = (bf16[128,256]{1,0:T(8,128)(2,1)S(1)}, bf16[128,256]{1,0:T(8,128)(2,1)S(1)}, u32[]{:S(2)}, u32[]{:S(2)}) collective-permute-start(bf16[128,256]{1,0:T(8,128)(2,1)S(1)} %get-tuple-element.7.kv_ref.kv0_ref), channel_id=1, source_target_pairs={{0,24},{8,32},{16,40},{24,48},{32,56},{40,64},{48,72},{56,80},{64,... | collective-permute-start | bytes 196616 | tf_op jit(solution)/shard_map/ppermute | solution.py:238
  38.2 5.9 %collective-permute-start.2 = (bf16[128,256]{1,0:T(8,128)(2,1)S(1)}, bf16[128,256]{1,0:T(8,128)(2,1)S(1)}, u32[]{:S(2)}, u32[]{:S(2)}) collective-permute-start(bf16[128,256]{1,0:T(8,128)(2,1)S(1)} %get-tuple-element.7.kv_ref.kv0_ref), channel_id=1, source_target_pairs={{0,16},{8,24},{16,32},{24,40},{32,48},{40,56},{48,64},{56,72},{64,... | collective-permute-start | bytes 196616 | tf_op jit(solution)/shard_map/ppermute | solution.py:238
  44.1 2.8 %collective-permute-start.1 = (bf16[128,256]{1,0:T(8,128)(2,1)S(1)}, bf16[128,256]{1,0:T(8,128)(2,1)S(1)}, u32[]{:S(2)}, u32[]{:S(2)}) collective-permute-start(bf16[128,256]{1,0:T(8,128)(2,1)S(1)} %get-tuple-element.7.kv_ref.kv0_ref), channel_id=1, source_target_pairs={{0,8},{8,16},{16,24},{24,32},{32,40},{40,48},{48,56},{56,64},{64,7... | collective-permute-start | bytes 196616 | tf_op jit(solution)/shard_map/ppermute | solution.py:238
  46.9 1.4 %shard_map.125 = (f32[128,1024]{1,0:T(8,128)S(1)}, f32[128,1024]{1,0:T(8,128)S(1)}) custom-call(s32[32]{0:T(128)S(1)} %copy-done.10, s32[1]{0:T(128)} %bitcast.begin_ref, f32[16]{0:T(128)S(1)} %copy-done.9, bf16[128,1024]{1,0:T(8,128)(2,1)S(1)} %copy-done.1, bf16[128,256]{1,0:T(8,128)(2,1)S(1)} %copy-done.3, bf16[128,256]{1,0:T(8,128)(2,1)S(1)} %copy-done.4, ...), custom_call_target="tpu_custom_call" | custom-call | flops 100000000 | bytes 1000000 | tf_op jit(solution)/shard_map/pallas_call | solution.py:257
  48.4 0.0 collective-permute-done.3.kv3_ref
  48.4 0.0 collective-permute-done.2.kv2_ref
  48.4 4.0 %collective-permute-done.1.kv1_ref = bf16[128,256]{1,0:T(8,128)(2,1)S(1)} collective-permute-done((bf16[128,256]{1,0:T(8,128)(2,1)S(1)}, bf16[128,256]{1,0:T(8,128)(2,1)S(1)}, u32[]{:S(2)}, u32[]{:S(2)}) %collective-permute-start.1) | collective-permute-done | bytes 65568 | tf_op jit(solution)/shard_map/ppermute | solution.py:238
  52.4 3.2 %shard_map.126.att_ref = bf16[128,1024]{1,0:T(8,128)(2,1)S(1)} custom-call(s32[32]{0:T(128)S(1)} %copy-done.10, s32[1]{0:T(128)} %bitcast.begin_ref, bf16[128,1024]{1,0:T(8,128)(2,1)S(1)} %copy-done.12, bf16[128,256]{1,0:T(8,128)(2,1)S(1)} %get-tuple-element.7.kv_ref.kv0_ref, bf16[128,256]{1,0:T(8,128)(2,1)S(1)} %collective-permute-done.1.kv1_ref, ...), custom_call_target="tpu_custom_call" | custom-call | flops 400000000 | bytes 1000000 | tf_op jit(solution)/shard_map/pallas_call | solution.py:265
  55.6 0.0 copy-start.8
  55.6 0.0 all-to-all-done.1.carried_ref
  55.6 0.7 copy-done.8
  56.3 0.3 shard_map.127
  56.6 14.7 %all_to_all.16.got_ref = bf16[8,16,2048]{2,1,0:T(8,128)(2,1)S(1)} all-to-all(bf16[8,16,2048]{2,1,0:T(8,128)(2,1)S(1)} %bitcast.4), channel_id=1, replica_groups=mesh['z'=16,'x'=4,'tp'=8] {'tp'}, dimensions={0} | all-to-all | bytes 1048576 | tf_op jit(solution)/shard_map/all_to_all | solution.py:282
  71.3 0.8 %shard_map.128 = (bf16[16,8192]{1,0:T(8,128)(2,1)}, bf16[16,8192]{1,0:T(8,128)(2,1)}) custom-call(bf16[8,16,2048]{2,1,0:T(8,128)(2,1)S(1)} %all_to_all.16.got_ref), custom_call_target="tpu_custom_call" | custom-call | bytes 1000000 | tf_op jit(solution)/shard_map/pallas_call | solution.py:283
  (13 shorter events, 0.0 us)
Async XLA Ops:
  0.6 0.7 copy-start.7
  0.6 0.7 copy-start.9
  0.7 0.7 copy-start.10
  1.3 1.0 %copy-start = (bf16[128,1024]{1,0:T(8,128)(2,1)S(1)}, bf16[128,1024]{1,0:T(8,128)(2,1)}, u32[]{:S(2)}) copy-start(bf16[128,1024]{1,0:T(8,128)(2,1)} %x_ref.3) | copy-start | bytes 786436
  2.3 0.8 %copy-start.2 = (bf16[128,256]{1,0:T(8,128)(2,1)S(1)}, bf16[128,256]{1,0:T(8,128)(2,1)}, u32[]{:S(2)}) copy-start(bf16[128,256]{1,0:T(8,128)(2,1)} %b_ref.3) | copy-start | bytes 196612
  3.1 0.8 %copy-start.5 = (bf16[128,128]{1,0:T(8,128)(2,1)S(1)}, bf16[128,128]{1,0:T(8,128)(2,1)}, u32[]{:S(2)}) copy-start(bf16[128,128]{1,0:T(8,128)(2,1)} %k_ref.1) | copy-start | bytes 98308
  3.9 0.8 %copy-start.6 = (bf16[128,128]{1,0:T(8,128)(2,1)S(1)}, bf16[128,128]{1,0:T(8,128)(2,1)}, u32[]{:S(2)}) copy-start(bf16[128,128]{1,0:T(8,128)(2,1)} %v_ref.1) | copy-start | bytes 98308
  20.2 8.2 %collective-permute-start = (bf16[384,256]{1,0:T(8,128)(2,1)S(1)}, bf16[384,256]{1,0:T(8,128)(2,1)S(1)}, u32[]{:S(2)}, u32[]{:S(2)}) collective-permute-start(bf16[384,256]{1,0:T(8,128)(2,1)S(1)} %shard_map.123), channel_id=1, source_target_pairs={{0,32},{32,64},{64,96},{96,128},{128,160},{160,192},{192,224},{224... | collective-permute-start | bytes 589832 | tf_op jit(solution)/shard_map/ppermute | solution.py:248
  29.4 17.5 %copy-start.1 = (bf16[128,1024]{1,0:T(8,128)(2,1)S(1)}, bf16[128,1024]{1,0:T(8,128)(2,1)}, u32[]{:S(2)}) copy-start(bf16[128,1024]{1,0:T(8,128)(2,1)} %x_ref.3) | copy-start | bytes 786436
  29.4 17.6 %copy-start.3 = (bf16[128,256]{1,0:T(8,128)(2,1)S(1)}, bf16[128,256]{1,0:T(8,128)(2,1)}, u32[]{:S(2)}) copy-start(bf16[128,256]{1,0:T(8,128)(2,1)} %b_ref.3) | copy-start | bytes 196612
  29.4 17.6 %copy-start.4 = (bf16[128,256]{1,0:T(8,128)(2,1)S(1)}, bf16[128,256]{1,0:T(8,128)(2,1)}, u32[]{:S(2)}) copy-start(bf16[128,256]{1,0:T(8,128)(2,1)} %c_ref.3) | copy-start | bytes 196612
  29.4 17.6 %copy-start.11 = (bf16[128,1024]{1,0:T(8,128)(2,1)S(1)}, bf16[128,1024]{1,0:T(8,128)(2,1)}, u32[]{:S(2)}) copy-start(bf16[128,1024]{1,0:T(8,128)(2,1)} %gate_ref.1) | copy-start | bytes 786436
  29.4 26.2 %all-to-all-start.1 = ((bf16[4,256,256]{2,1,0:T(8,128)(2,1)}), bf16[4,256,256]{2,1,0:T(8,128)(2,1)S(1)}, u32[]{:S(2)}, u32[]{:S(2)}) async-start(bf16[4,256,256]{2,1,0:T(8,128)(2,1)} %shard_map.124), calls=%async_computation.1 | async-start | bytes 1048576 | tf_op jit(solution)/shard_map/all_to_all | solution.py:256
  33.0 19.4 %copy-start.12 = (bf16[128,1024]{1,0:T(8,128)(2,1)S(1)}, bf16[128,1024]{1,0:T(8,128)(2,1)}, u32[]{:S(2)}) copy-start(bf16[128,1024]{1,0:T(8,128)(2,1)} %q_ref.1) | copy-start | bytes 786436
  33.0 15.4 %collective-permute-start.3 = (bf16[128,256]{1,0:T(8,128)(2,1)S(1)}, bf16[128,256]{1,0:T(8,128)(2,1)S(1)}, u32[]{:S(2)}, u32[]{:S(2)}) collective-permute-start(bf16[128,256]{1,0:T(8,128)(2,1)S(1)} %get-tuple-element.7.kv_ref.kv0_ref), channel_id=1, source_target_pairs={{0,24},{8,32},{16,40},{24,48},{32,56},{40,64},{48,72},{56,80},{64,... | collective-permute-start | bytes 196616 | tf_op jit(solution)/shard_map/ppermute | solution.py:238
  38.2 10.2 %collective-permute-start.2 = (bf16[128,256]{1,0:T(8,128)(2,1)S(1)}, bf16[128,256]{1,0:T(8,128)(2,1)S(1)}, u32[]{:S(2)}, u32[]{:S(2)}) collective-permute-start(bf16[128,256]{1,0:T(8,128)(2,1)S(1)} %get-tuple-element.7.kv_ref.kv0_ref), channel_id=1, source_target_pairs={{0,16},{8,24},{16,32},{24,40},{32,48},{40,56},{48,64},{56,72},{64,... | collective-permute-start | bytes 196616 | tf_op jit(solution)/shard_map/ppermute | solution.py:238
  44.1 8.3 %collective-permute-start.1 = (bf16[128,256]{1,0:T(8,128)(2,1)S(1)}, bf16[128,256]{1,0:T(8,128)(2,1)S(1)}, u32[]{:S(2)}, u32[]{:S(2)}) collective-permute-start(bf16[128,256]{1,0:T(8,128)(2,1)S(1)} %get-tuple-element.7.kv_ref.kv0_ref), channel_id=1, source_target_pairs={{0,8},{8,16},{16,24},{24,32},{32,40},{40,48},{48,56},{56,64},{64,7... | collective-permute-start | bytes 196616 | tf_op jit(solution)/shard_map/ppermute | solution.py:238
  55.6 0.7 copy-start.8

commit v2 on v1

--- a/solution.py
+++ b/solution.py
@@ -19,15 +19,18 @@
 BF16 = jnp.bfloat16
 VMEM = pl.BlockSpec(memory_space=pltpu.VMEM)
 SMEM = pl.BlockSpec(memory_space=pltpu.SMEM)
-
-
-def call(kernel, outs, specs, flops=0, moved=0, exps=0):
+HBM = pl.BlockSpec(memory_space=pltpu.HBM)
+LATER = pl.BlockSpec(memory_space=pl.ANY)
+
+
+def call(kernel, outs, specs, flops=0, moved=0, exps=0, scratch=(), grant=32 * 2**20):
     return pl.pallas_call(
         kernel,
         out_shape=outs,
         in_specs=specs,
+        scratch_shapes=scratch,
         out_specs=jax.tree.map(lambda _: VMEM, outs),
-        compiler_params=pltpu.CompilerParams(vmem_limit_bytes=32 * 2**20),
+        compiler_params=pltpu.CompilerParams(vmem_limit_bytes=grant),
         cost_estimate=pl.CostEstimate(flops=flops, bytes_accessed=moved, transcendentals=exps),
     )
 
@@ -85,14 +88,46 @@
     return sum(dot(part, pick, ((0,), (0,))) for part in parts)
 
 
-def prepare(doc_ref, begin_ref, rate_ref, x_ref, b_ref, dt_ref, k_ref, v_ref, out_ref, kv_ref):
+def prepare(
+    begin_ref,
+    doc_hbm,
+    rate_hbm,
+    dt_hbm,
+    x_hbm,
+    b_hbm,
+    k_hbm,
+    v_hbm,
+    out_ref,
+    kv_ref,
+    doc_ref,
+    rate_ref,
+    dt_ref,
+    x_ref,
+    b_ref,
+    sems,
+):
+    pairs = (
+        (doc_hbm, doc_ref),
+        (rate_hbm, rate_ref),
+        (dt_hbm, dt_ref),
+        (x_hbm, x_ref),
+        (b_hbm, b_ref),
+        (k_hbm, kv_ref.at[:, :ROWS]),
+        (v_hbm, kv_ref.at[:, ROWS:]),
+    )
+    copies = [pltpu.make_async_copy(s, d, sems.at[i]) for i, (s, d) in enumerate(pairs)]
+    for copy in copies:
+        copy.start()
     begin = begin_ref[0]
+    for copy in copies[:3]:
+        copy.wait()
     _, last_start = start_row(doc_ref, begin)
     dt, total = head_rows(dt_ref, rate_ref)
     final = total[:, ROWS - 1 :]
     pos = begin + lax.broadcasted_iota(jnp.int32, (GROUP_HEADS, ROWS), 1)
     tail = jnp.where(pos >= last_start, jnp.exp(final - total) * dt, 0.0)
     tail = spread_heads(three_parts(tail))
+    copies[3].wait()
     scaled = (x_ref[...].astype(F32) * tail).astype(BF16)
     whole = jnp.broadcast_to(final, (GROUP_HEADS, ROWS))
     transmit = jnp.where(last_start < begin, jnp.exp(whole), 0.0)
@@ -103,13 +138,14 @@
         parts[0].astype(F32),
         jnp.where(row == 1, parts[1].astype(F32), parts[2].astype(F32)),
     ).astype(BF16)
+    copies[4].wait()
     state = dot(b_ref[...], scaled, ((0,), (0,))).astype(BF16)
     width = GROUP_HEADS * HALF // PEERS
     for j in range(PEERS):
         out_ref[j, :STATE, :] = state[:, j * width : (j + 1) * width]
         out_ref[j, STATE:, :] = sent[:, j * width : (j + 1) * width]
-    kv_ref[:, :ROWS] = k_ref[...]
-    kv_ref[:, ROWS:] = v_ref[...]
+    for copy in copies[5:]:
+        copy.wait()
 
 
 def received(ref, j):
@@ -118,7 +154,13 @@
     return state, parts[0:1] + parts[1:2] + parts[2:3]
 
 
-def group_state(got_ref, kv_ref, out_ref):
+def pair_up(kv_ref, near_ref, pair_ref):
+    pair_ref[:ROWS, :] = kv_ref[...]
+    pair_ref[ROWS:, :] = near_ref[...]
+
+
+def group_state(got_ref, kv_ref, near_ref, out_ref):
+    del near_ref
     total, _ = received(got_ref, 0)
     for j in range(1, PEERS):
         state, transmit = received(got_ref, j)
@@ -141,8 +183,24 @@
     return jnp.transpose(jnp.broadcast_to(found[:1].astype(F32), (ROWS, ROWS)))
 
 
-def inside(doc_ref, begin_ref, rate_ref, x_ref, b_ref, c_ref, dt_ref, gate_ref, own_ref, factor_ref):
+def inside(
+    begin_ref,
+    doc_ref,
+    rate_ref,
+    x_ref,
+    b_ref,
+    c_ref,
+    dt_ref,
+    gate_ref,
+    gain_ref,
+    carried_ref,
+    own_ref,
+    factor_ref,
+    gain_out_ref,
+):
+    del carried_ref
     begin = begin_ref[0]
+    gain_out_ref[...] = gain_ref[...]
     starts = start_columns(doc_ref, begin)
     row = lax.broadcasted_iota(jnp.int32, (ROWS, ROWS), 0)
     lane = lax.broadcasted_iota(jnp.int32, (ROWS, ROWS), 1)
@@ -171,12 +229,12 @@
         factor_ref[:, at] = entry * gate
 
 
-def attention(doc_ref, begin_ref, q_ref, kv0_ref, kv1_ref, kv2_ref, kv3_ref, kv4_ref, out_ref):
+def attention(begin_ref, doc_ref, q_ref, kv0_ref, kv1_ref, pair_ref, kv4_ref, out_ref):
     begin = begin_ref[0]
     starts = start_columns(doc_ref, begin)
     row = lax.broadcasted_iota(jnp.int32, (ROWS, ROWS), 0)
     lane = lax.broadcasted_iota(jnp.int32, (ROWS, ROWS), 1)
-    blocks = [kv0_ref[...], kv1_ref[...], kv2_ref[...], kv3_ref[...], kv4_ref[STATE:, :]]
+    blocks = [kv0_ref[...], kv1_ref[...], pair_ref[:ROWS, :], pair_ref[ROWS:, :], kv4_ref[STATE:, :]]
     bias = []
     for j in range(len(blocks)):
         allowed = (begin - j * ROWS + lane).astype(F32) >= starts
@@ -227,24 +285,35 @@
     own_states, kv = call(
         prepare,
         (shaped((PEERS, STATE + 16, width // PEERS), BF16), shaped((ROWS, 2 * ROWS), BF16)),
-        [SMEM, SMEM, SMEM] + [VMEM] * 5,
+        [SMEM] + [HBM] * 7,
         flops=10**8,
         moved=10**6,
-    )(doc, begin, rate, x, b, dt, k, v)
+        scratch=(
+            pltpu.SMEM(doc.shape, jnp.int32),
+            pltpu.SMEM(rate.shape, F32),
+            pltpu.VMEM(dt.shape, F32),
+            pltpu.VMEM(x.shape, BF16),
+            pltpu.VMEM(b.shape, BF16),
+            pltpu.SemaphoreType.DMA((7,)),
+        ),
+        grant=None,
+    )(begin, doc, rate, dt, x, b, k, v)
     got = lax.all_to_all(own_states, "x", 0, 0, tiled=True)
 
     def along(a, distance):
         count = lax.axis_size("z") * PEERS
         return lax.ppermute(a, ("z", "x"), [(i - distance, i) for i in range(distance, count)])
 
-    near = [along(kv, d) for d in range(1, PEERS)]
+    kv1 = along(kv, 1)
+    pair = call(pair_up, shaped((2 * ROWS, 2 * ROWS), BF16), [VMEM] * 2, moved=10**8)(kv, kv1)
+    pair = along(pair, 2)
     group = call(
         group_state,
         shaped((STATE + ROWS, width // PEERS), BF16),
-        [VMEM] * 2,
+        [VMEM] * 2 + [LATER],
         flops=10**6,
         moved=10**6,
-    )(got, kv)
+    )(got, kv, kv1)
     before = lax.ppermute(group, "z", [(i - 1, i) for i in range(1, lax.axis_size("z"))])
     carried = call(
         carried_states,
@@ -253,23 +322,23 @@
         flops=10**6,
         moved=10**6,
     )(got, before)
+    own, factor, gain = call(
+        inside,
+        (shaped((ROWS, width), F32), shaped((ROWS, width), F32), shaped((1, width), F32)),
+        [SMEM, SMEM, SMEM] + [VMEM] * 6 + [LATER],
+        flops=10**8,
+        moved=10**6,
+        exps=400000,
+    )(begin, doc, rate, x, b, c, dt, gate, weight.reshape(1, width), carried)
     carried = lax.all_to_all(carried, "x", 0, 0, tiled=True)
-    own, factor = call(
-        inside,
-        (shaped((ROWS, width), F32), shaped((ROWS, width), F32)),
-        [SMEM, SMEM, SMEM] + [VMEM] * 5,
-        flops=10**8,
-        moved=10**6,
-        exps=400000,
-    )(doc, begin, rate, x, b, c, dt, gate)
     att = call(
         attention,
         shaped((ROWS, width), BF16),
-        [SMEM, SMEM] + [VMEM] * 6,
-        flops=4 * 10**8,
-        moved=10**6,
-        exps=700000,
-    )(doc, begin, q, kv, *near, before)
+        [SMEM, SMEM] + [VMEM] * 5,
+        flops=10**10,
+        moved=10**8,
+        exps=10**8,
+    )(begin, doc, q, kv, kv1, pair, before)
     rows = pl.pallas_call(
         finish,
         out_shape=shaped((ROWS, 2 * width), BF16),
@@ -278,7 +347,7 @@
         scratch_shapes=[pltpu.VMEM((ROWS, width), F32)],
         compiler_params=pltpu.CompilerParams(vmem_limit_bytes=32 * 2**20),
         cost_estimate=pl.CostEstimate(flops=10**8, bytes_accessed=10**6, transcendentals=128),
-    )(c, carried, own, factor, weight.reshape(1, width), att)
+    )(c, carried, own, factor, gain, att)
     moved = lax.all_to_all(rows.reshape(tp, ROWS // tp, 2 * width), "tp", 0, 0, tiled=True)
     return call(
         lay_out,

time: 72.7 us -> 57.6 us (0.79)
  the two profiles are of different devices: /device:TPU:224 before, /device:TPU:64 now
where the time goes in v2:
time: 57.6 us; the launch traced here: 57.2 us
  starting transfers between devices  20.7 us (36%)
  blocking collectives  14.7 us (26%)
  waiting for transfers between devices  10.7 us (19%)
  Pallas kernels  9.72 us (17%)
  between operations  0.82 us (1%)
  local copies, waits for them, and re-layouts  0.63 us (1%)
    all_to_all x1, blocking collectives, local(): lax.all_to_all(rows.reshape(tp, ROWS // tp, 2 * width), 'tp', 0, 0, tiled...  14.7 us
    ppermute x2, starting transfers between devices, along(): lax.ppermute(a, ('z', 'x'), [(i - distance, i) for i in range(distance, c...  6.69 us
    all_to_all x1, starting transfers between devices, local(): carried = lax.all_to_all(carried, 'x', 0, 0, tiled=True)  5.71 us
    ppermute x2, waiting for transfers between devices, along(): lax.ppermute(a, ('z', 'x'), [(i - distance, i) for i in range(distance, c...  4.77 us
    all_to_all x1, starting transfers between devices, local(): got = lax.all_to_all(own_states, 'x', 0, 0, tiled=True)  4.44 us
    ppermute x1, starting transfers between devices, local(): lax.ppermute(group, 'z', [(i - 1, i) for i in range(1, lax.axis_size('z'))])  3.82 us
    pallas_call x1, Pallas kernels, local(): call(attention, shaped((ROWS, width), BF16), [SMEM, SMEM] + [VMEM] * 5, f...  3.12 us
    pallas_call x1, Pallas kernels, local(): call(prepare, (shaped((PEERS, STATE + 16, width // PEERS), BF16), shaped(...  2.96 us
  transfers between devices with their start and end apart: 5, of which 4 were waited for; matrix products, arithmetic and copies ran while one was open for 0% of the time, Pallas kernels for 10%

profile of v2, /device:TPU:64, one launch (start us, length us, event | category | flops | bytes accessed | tf_op | source)
XLA Modules:
  0.0 57.2 jit_solution(15735794212110168020)
XLA Ops:
  0.6 3.0 %shard_map.122 = (bf16[4,272,256]{2,1,0:T(8,128)(2,1)}, bf16[128,256]{1,0:T(8,128)(2,1)}) custom-call(s32[1]{0:T(128)} %bitcast.begin_ref, s32[32]{0:T(128)} %doc_ref.3, f32[16]{0:T(128)} %rate_ref.1, f32[16,128]{1,0:T(8,128)} %bitcast.5, bf16[128,1024]{1,0:T(8,128)(2,1)} %x_ref.1, bf16[128,256]{1,0:T(8,128)(2,1)} %b_ref.1, bf16[128,128]{1,0:T(8,128)(2,1)} %k_hbm.1, ...), custom_call_target="tpu_custom_call" | custom-call | flops 100000000 | bytes 1000000 | tf_op jit(solution)/shard_map/pallas_call | solution.py:285
  3.6 0.0 copy-start.4
  3.6 4.4 %all-to-all-start = ((bf16[4,272,256]{2,1,0:T(8,128)(2,1)}), bf16[4,272,256]{2,1,0:T(8,128)(2,1)S(1)}, u32[]{:S(2)}, u32[]{:S(2)}) async-start(bf16[4,272,256]{2,1,0:T(8,128)(2,1)} %get-tuple-element.7), calls=%async_computation | async-start | bytes 1114112 | tf_op jit(solution)/shard_map/all_to_all | solution.py:301
  8.1 0.0 copy-done.4
  8.1 3.9 %collective-permute-start = (bf16[128,256]{1,0:T(8,128)(2,1)S(1)}, bf16[128,256]{1,0:T(8,128)(2,1)S(1)}, u32[]{:S(2)}, u32[]{:S(2)}) collective-permute-start(bf16[128,256]{1,0:T(8,128)(2,1)S(1)} %copy-done.4), channel_id=1, source_target_pairs={{0,8},{8,16},{16,24},{24,32},{32,40},{40,48},{48,56},{56,64},{64,7... | collective-permute-start | bytes 196616 | tf_op jit(solution)/shard_map/ppermute | solution.py:305
  12.0 4.8 %collective-permute-done.near_ref.kv1_ref = bf16[128,256]{1,0:T(8,128)(2,1)S(1)} collective-permute-done((bf16[128,256]{1,0:T(8,128)(2,1)S(1)}, bf16[128,256]{1,0:T(8,128)(2,1)S(1)}, u32[]{:S(2)}, u32[]{:S(2)}) %collective-permute-start) | collective-permute-done | bytes 65568 | tf_op jit(solution)/shard_map/ppermute | solution.py:305
  16.8 2.2 %all-to-all-done.got_ref = bf16[4,272,256]{2,1,0:T(8,128)(2,1)S(1)} async-done(((bf16[4,272,256]{2,1,0:T(8,128)(2,1)}), bf16[4,272,256]{2,1,0:T(8,128)(2,1)S(1)}, u32[]{:S(2)}, u32[]{:S(2)}) %all-to-all-start) | async-done | bytes 557088 | tf_op jit(solution)/shard_map/all_to_all | solution.py:301
  19.0 0.1 shard_map.123
  19.1 3.8 %collective-permute-start.1 = (bf16[384,256]{1,0:T(8,128)(2,1)S(1)}, bf16[384,256]{1,0:T(8,128)(2,1)S(1)}, u32[]{:S(2)}, u32[]{:S(2)}) collective-permute-start(bf16[384,256]{1,0:T(8,128)(2,1)S(1)} %shard_map.123), channel_id=1, source_target_pairs={{0,32},{32,64},{64,96},{96,128},{128,160},{160,192},{192,224},{224... | collective-permute-start | bytes 589832 | tf_op jit(solution)/shard_map/ppermute | solution.py:317
  23.0 2.8 %collective-permute-start.2 = (bf16[256,256]{1,0:T(8,128)(2,1)S(1)}, bf16[256,256]{1,0:T(8,128)(2,1)S(1)}, u32[]{:S(2)}, u32[]{:S(2)}) collective-permute-start(bf16[256,256]{1,0:T(8,128)(2,1)S(1)} %shard_map.126), channel_id=1, source_target_pairs={{0,16},{8,24},{16,32},{24,40},{32,48},{40,56},{48,64},{56,72},{64,... | collective-permute-start | bytes 393224 | tf_op jit(solution)/shard_map/ppermute | solution.py:305
  25.7 0.9 %collective-permute-done.1.before_ref.kv4_ref = bf16[384,256]{1,0:T(8,128)(2,1)S(1)} collective-permute-done((bf16[384,256]{1,0:T(8,128)(2,1)S(1)}, bf16[384,256]{1,0:T(8,128)(2,1)S(1)}, u32[]{:S(2)}, u32[]{:S(2)}) %collective-permute-start.1) | collective-permute-done | bytes 196640 | tf_op jit(solution)/shard_map/ppermute | solution.py:317
  26.7 0.9 %shard_map.124.carried_ref = bf16[4,256,256]{2,1,0:T(8,128)(2,1)} custom-call(bf16[4,272,256]{2,1,0:T(8,128)(2,1)S(1)} %all-to-all-done.got_ref, bf16[384,256]{1,0:T(8,128)(2,1)S(1)} %collective-permute-done.1.before_ref.kv4_ref), custom_call_target="tpu_custom_call" | custom-call | flops 1000000 | bytes 1000000 | tf_op jit(solution)/shard_map/pallas_call | solution.py:318
  27.6 5.7 %all-to-all-start.1 = ((bf16[4,256,256]{2,1,0:T(8,128)(2,1)}), bf16[4,256,256]{2,1,0:T(8,128)(2,1)S(1)}, u32[]{:S(2)}, u32[]{:S(2)}) async-start(bf16[4,256,256]{2,1,0:T(8,128)(2,1)} %shard_map.124.carried_ref), calls=%async_computation.1 | async-start | bytes 1048576 | tf_op jit(solution)/shard_map/all_to_all | solution.py:333
  33.3 0.0 copy-start.3
  33.3 0.0 copy-start.5
  33.3 0.0 collective-permute-done.2.pair_ref
  33.3 0.0 copy-done.7
  33.4 0.0 copy-start.6
  33.4 3.1 %shard_map.127.att_ref = bf16[128,1024]{1,0:T(8,128)(2,1)S(1)} custom-call(s32[1]{0:T(128)} %bitcast.begin_ref, s32[32]{0:T(128)S(1)} %copy-done.7, bf16[128,1024]{1,0:T(8,128)(2,1)S(1)} %copy-done.9, bf16[128,256]{1,0:T(8,128)(2,1)S(1)} %copy-done.4, bf16[128,256]{1,0:T(8,128)(2,1)S(1)} %collective-permute-done.near_ref.kv1_ref, ...), custom_call_target="tpu_custom_call" | custom-call | flops 10000000000 | bytes 100000000 | tf_op jit(solution)/shard_map/pallas_call | solution.py:334
  36.5 0.0 copy-start.8
  36.5 0.0 copy-done
  36.5 0.0 copy-done.1
  36.5 0.0 copy-done.2
  36.5 0.0 copy-done.3
  36.6 0.0 copy-done.5
  36.6 0.0 copy-done.6
  36.6 0.6 %copy-done.8 = f32[16]{0:T(128)S(1)} copy-done((f32[16]{0:T(128)S(1)}, f32[16]{0:T(128)}, u32[]{:S(2)}) %copy-start.8) | copy-done | bytes 88
  37.2 1.4 %shard_map.125 = (f32[128,1024]{1,0:T(8,128)S(1)}, f32[128,1024]{1,0:T(8,128)S(1)}, f32[1,1024]{1,0:T(1,128)S(1)}) custom-call(s32[1]{0:T(128)} %bitcast.begin_ref, s32[32]{0:T(128)S(1)} %copy-done.7, f32[16]{0:T(128)S(1)} %copy-done.8, bf16[128,1024]{1,0:T(8,128)(2,1)S(1)} %copy-done, bf16[128,256]{1,0:T(8,128)(2,1)S(1)} %copy-done.2, ...), custom_call_target="tpu_custom_call" | custom-call | flops 100000000 | bytes 1000000 | tf_op jit(solution)/shard_map/pallas_call | solution.py:325
  38.6 2.8 %all-to-all-done.1.carried_ref = bf16[4,256,256]{2,1,0:T(8,128)(2,1)S(1)} async-done(((bf16[4,256,256]{2,1,0:T(8,128)(2,1)}), bf16[4,256,256]{2,1,0:T(8,128)(2,1)S(1)}, u32[]{:S(2)}, u32[]{:S(2)}) %all-to-all-start.1) | async-done | bytes 524320 | tf_op jit(solution)/shard_map/all_to_all | solution.py:333
  41.4 0.3 shard_map.128
  41.7 14.7 %all_to_all.15.got_ref = bf16[8,16,2048]{2,1,0:T(8,128)(2,1)S(1)} all-to-all(bf16[8,16,2048]{2,1,0:T(8,128)(2,1)S(1)} %bitcast.4), channel_id=1, replica_groups=mesh['z'=16,'x'=4,'tp'=8] {'tp'}, dimensions={0} | all-to-all | bytes 1048576 | tf_op jit(solution)/shard_map/all_to_all | solution.py:351
  56.4 0.8 %shard_map.129 = (bf16[16,8192]{1,0:T(8,128)(2,1)}, bf16[16,8192]{1,0:T(8,128)(2,1)}) custom-call(bf16[8,16,2048]{2,1,0:T(8,128)(2,1)S(1)} %all_to_all.15.got_ref), custom_call_target="tpu_custom_call" | custom-call | bytes 1000000 | tf_op jit(solution)/shard_map/pallas_call | solution.py:352
  (7 shorter events, 0.0 us)
Async XLA Ops:
  3.6 4.5 %copy-start.4 = (bf16[128,256]{1,0:T(8,128)(2,1)S(1)}, bf16[128,256]{1,0:T(8,128)(2,1)}, u32[]{:S(2)}) copy-start(bf16[128,256]{1,0:T(8,128)(2,1)} %get-tuple-element.8.kv_ref.kv0_ref) | copy-start | bytes 196612
  3.6 15.4 %all-to-all-start = ((bf16[4,272,256]{2,1,0:T(8,128)(2,1)}), bf16[4,272,256]{2,1,0:T(8,128)(2,1)S(1)}, u32[]{:S(2)}, u32[]{:S(2)}) async-start(bf16[4,272,256]{2,1,0:T(8,128)(2,1)} %get-tuple-element.7), calls=%async_computation | async-start | bytes 1114112 | tf_op jit(solution)/shard_map/all_to_all | solution.py:301
  8.1 8.7 %collective-permute-start = (bf16[128,256]{1,0:T(8,128)(2,1)S(1)}, bf16[128,256]{1,0:T(8,128)(2,1)S(1)}, u32[]{:S(2)}, u32[]{:S(2)}) collective-permute-start(bf16[128,256]{1,0:T(8,128)(2,1)S(1)} %copy-done.4), channel_id=1, source_target_pairs={{0,8},{8,16},{16,24},{24,32},{32,40},{40,48},{48,56},{56,64},{64,7... | collective-permute-start | bytes 196616 | tf_op jit(solution)/shard_map/ppermute | solution.py:305
  19.1 7.6 %collective-permute-start.1 = (bf16[384,256]{1,0:T(8,128)(2,1)S(1)}, bf16[384,256]{1,0:T(8,128)(2,1)S(1)}, u32[]{:S(2)}, u32[]{:S(2)}) collective-permute-start(bf16[384,256]{1,0:T(8,128)(2,1)S(1)} %shard_map.123), channel_id=1, source_target_pairs={{0,32},{32,64},{64,96},{96,128},{128,160},{160,192},{192,224},{224... | collective-permute-start | bytes 589832 | tf_op jit(solution)/shard_map/ppermute | solution.py:317
  23.0 10.4 %collective-permute-start.2 = (bf16[256,256]{1,0:T(8,128)(2,1)S(1)}, bf16[256,256]{1,0:T(8,128)(2,1)S(1)}, u32[]{:S(2)}, u32[]{:S(2)}) collective-permute-start(bf16[256,256]{1,0:T(8,128)(2,1)S(1)} %shard_map.126), channel_id=1, source_target_pairs={{0,16},{8,24},{16,32},{24,40},{32,48},{40,56},{48,64},{56,72},{64,... | collective-permute-start | bytes 393224 | tf_op jit(solution)/shard_map/ppermute | solution.py:305
  27.6 5.8 %copy-start.7 = (s32[32]{0:T(128)S(1)}, s32[32]{0:T(128)}, u32[]{:S(2)}) copy-start(s32[32]{0:T(128)} %doc_ref.3) | copy-start | bytes 388
  27.6 5.8 %copy-start.9 = (bf16[128,1024]{1,0:T(8,128)(2,1)S(1)}, bf16[128,1024]{1,0:T(8,128)(2,1)}, u32[]{:S(2)}) copy-start(bf16[128,1024]{1,0:T(8,128)(2,1)} %q_ref.1) | copy-start | bytes 786436
  27.6 13.8 %all-to-all-start.1 = ((bf16[4,256,256]{2,1,0:T(8,128)(2,1)}), bf16[4,256,256]{2,1,0:T(8,128)(2,1)S(1)}, u32[]{:S(2)}, u32[]{:S(2)}) async-start(bf16[4,256,256]{2,1,0:T(8,128)(2,1)} %shard_map.124.carried_ref), calls=%async_computation.1 | async-start | bytes 1048576 | tf_op jit(solution)/shard_map/all_to_all | solution.py:333
  33.3 3.2 %copy-start = (bf16[128,1024]{1,0:T(8,128)(2,1)S(1)}, bf16[128,1024]{1,0:T(8,128)(2,1)}, u32[]{:S(2)}) copy-start(bf16[128,1024]{1,0:T(8,128)(2,1)} %x_ref.1) | copy-start | bytes 786436
  33.3 3.2 %copy-start.1 = (bf16[128,1024]{1,0:T(8,128)(2,1)S(1)}, bf16[128,1024]{1,0:T(8,128)(2,1)}, u32[]{:S(2)}) copy-start(bf16[128,1024]{1,0:T(8,128)(2,1)} %gate_ref.1) | copy-start | bytes 786436
  33.3 3.2 %copy-start.2 = (bf16[128,256]{1,0:T(8,128)(2,1)S(1)}, bf16[128,256]{1,0:T(8,128)(2,1)}, u32[]{:S(2)}) copy-start(bf16[128,256]{1,0:T(8,128)(2,1)} %b_ref.1) | copy-start | bytes 196612
  33.3 3.2 %copy-start.3 = (bf16[128,256]{1,0:T(8,128)(2,1)S(1)}, bf16[128,256]{1,0:T(8,128)(2,1)}, u32[]{:S(2)}) copy-start(bf16[128,256]{1,0:T(8,128)(2,1)} %c_ref.3) | copy-start | bytes 196612
  33.3 3.2 %copy-start.5 = (f32[128,16]{0,1:T(8,128)S(1)}, f32[128,16]{0,1:T(8,128)}, u32[]{:S(2)}) copy-start(f32[128,16]{0,1:T(8,128)} %param.16) | copy-start | bytes 24580
  33.4 3.2 %copy-start.6 = (f32[1024]{0:T(1024)S(1)}, f32[1024]{0:T(1024)}, u32[]{:S(2)}) copy-start(f32[1024]{0:T(1024)} %param.18) | copy-start | bytes 12292
  36.5 0.7 %copy-start.8 = (f32[16]{0:T(128)S(1)}, f32[16]{0:T(128)}, u32[]{:S(2)}) copy-start(f32[16]{0:T(128)} %rate_ref.1) | copy-start | bytes 196

commit v3 on v2

--- a/solution.py
+++ b/solution.py
@@ -23,13 +23,13 @@
 LATER = pl.BlockSpec(memory_space=pl.ANY)
 
 
-def call(kernel, outs, specs, flops=0, moved=0, exps=0, scratch=(), grant=32 * 2**20):
+def call(kernel, outs, specs, flops=0, moved=0, exps=0, scratch=(), grant=32 * 2**20, out=VMEM):
     return pl.pallas_call(
         kernel,
         out_shape=outs,
         in_specs=specs,
         scratch_shapes=scratch,
-        out_specs=jax.tree.map(lambda _: VMEM, outs),
+        out_specs=jax.tree.map(lambda _: out, outs),
         compiler_params=pltpu.CompilerParams(vmem_limit_bytes=grant),
         cost_estimate=pl.CostEstimate(flops=flops, bytes_accessed=moved, transcendentals=exps),
     )
@@ -74,18 +74,18 @@
     upto = lax.broadcasted_iota(jnp.int32, (ROWS, ROWS), 0) <= lax.broadcasted_iota(
         jnp.int32, (ROWS, ROWS), 1
     )
-    decay = -(dt * rate)
     upto = upto.astype(F32).astype(BF16)
-    total = sum(dot(part, upto) for part in three_parts(decay))
+    sums = dot(jnp.concatenate(three_parts(-(dt * rate)), 0), upto)
+    total = sums[:GROUP_HEADS] + sums[GROUP_HEADS : 2 * GROUP_HEADS] + sums[2 * GROUP_HEADS :]
     return dt, total
 
 
-def spread_heads(parts):
+def spread_heads(a):
     width = GROUP_HEADS * HALF
-    lane = lax.broadcasted_iota(jnp.int32, (GROUP_HEADS, width), 1)
-    row = lax.broadcasted_iota(jnp.int32, (GROUP_HEADS, width), 0)
+    lane = lax.broadcasted_iota(jnp.int32, (3 * GROUP_HEADS, width), 1)
+    row = lax.broadcasted_iota(jnp.int32, (3 * GROUP_HEADS, width), 0) & (GROUP_HEADS - 1)
     pick = ((lane >= row * HALF) & (lane < (row + 1) * HALF)).astype(F32).astype(BF16)
-    return sum(dot(part, pick, ((0,), (0,))) for part in parts)
+    return dot(jnp.concatenate(three_parts(a), 0), pick, ((0,), (0,)))
 
 
 def prepare(
@@ -97,26 +97,33 @@
     b_hbm,
     k_hbm,
     v_hbm,
-    out_ref,
-    kv_ref,
+    out_hbm,
+    kv_hbm,
     doc_ref,
     rate_ref,
     dt_ref,
     x_ref,
     b_ref,
+    kv_ref,
+    out_ref,
     sems,
 ):
     pairs = (
         (doc_hbm, doc_ref),
         (rate_hbm, rate_ref),
         (dt_hbm, dt_ref),
+        (b_hbm, b_ref),
         (x_hbm, x_ref),
-        (b_hbm, b_ref),
         (k_hbm, kv_ref.at[:, :ROWS]),
         (v_hbm, kv_ref.at[:, ROWS:]),
+        (kv_ref, kv_hbm),
+        (out_ref.at[0], out_hbm.at[0]),
+        (out_ref.at[1], out_hbm.at[1]),
+        (out_ref.at[2], out_hbm.at[2]),
+        (out_ref.at[3], out_hbm.at[3]),
     )
     copies = [pltpu.make_async_copy(s, d, sems.at[i]) for i, (s, d) in enumerate(pairs)]
-    for copy in copies:
+    for copy in copies[:7]:
         copy.start()
     begin = begin_ref[0]
     for copy in copies[:3]:
@@ -126,25 +133,30 @@
     final = total[:, ROWS - 1 :]
     pos = begin + lax.broadcasted_iota(jnp.int32, (GROUP_HEADS, ROWS), 1)
     tail = jnp.where(pos >= last_start, jnp.exp(final - total) * dt, 0.0)
-    tail = spread_heads(three_parts(tail))
-    copies[3].wait()
-    scaled = (x_ref[...].astype(F32) * tail).astype(BF16)
+    tail = spread_heads(tail)
     whole = jnp.broadcast_to(final, (GROUP_HEADS, ROWS))
     transmit = jnp.where(last_start < begin, jnp.exp(whole), 0.0)
-    parts = three_parts(spread_heads([p[:, :16] for p in three_parts(transmit)]))
+    parts = three_parts(spread_heads(transmit)[:16])
     row = lax.broadcasted_iota(jnp.int32, (16, GROUP_HEADS * HALF), 0)
     sent = jnp.where(
         row == 0,
         parts[0].astype(F32),
         jnp.where(row == 1, parts[1].astype(F32), parts[2].astype(F32)),
     ).astype(BF16)
+    copies[3].wait()
+    turned = jnp.transpose(b_ref[...])
     copies[4].wait()
-    state = dot(b_ref[...], scaled, ((0,), (0,))).astype(BF16)
     width = GROUP_HEADS * HALF // PEERS
     for j in range(PEERS):
-        out_ref[j, :STATE, :] = state[:, j * width : (j + 1) * width]
-        out_ref[j, STATE:, :] = sent[:, j * width : (j + 1) * width]
-    for copy in copies[5:]:
+        at = slice(j * width, (j + 1) * width)
+        scaled = (x_ref[:, at].astype(F32) * tail[:, at]).astype(BF16)
+        out_ref[j, :STATE, :] = dot(turned, scaled).astype(BF16)
+        out_ref[j, STATE:, :] = sent[:, at]
+        copies[8 + j].start()
+    for copy in copies[5:7]:
+        copy.wait()
+    copies[7].start()
+    for copy in copies[7:]:
         copy.wait()
 
 
@@ -169,13 +181,18 @@
     out_ref[STATE:, :] = kv_ref[...]
 
 
-def carried_states(got_ref, before_ref, out_ref):
+def carried_states(got_ref, before_ref, out_hbm, out_ref, sems):
     carried = before_ref[:STATE, :].astype(F32)
+    copies = []
     for j in range(PEERS):
         out_ref[j] = carried.astype(BF16)
+        copies.append(pltpu.make_async_copy(out_ref.at[j], out_hbm.at[j], sems.at[j]))
+        copies[j].start()
         if j < PEERS - 1:
             state, transmit = received(got_ref, j)
             carried = carried * transmit + state
+    for copy in copies:
+        copy.wait()
 
 
 def start_columns(doc_ref, begin):
@@ -294,9 +311,12 @@
             pltpu.VMEM(dt.shape, F32),
             pltpu.VMEM(x.shape, BF16),
             pltpu.VMEM(b.shape, BF16),
-            pltpu.SemaphoreType.DMA((7,)),
+            pltpu.VMEM((ROWS, 2 * ROWS), BF16),
+            pltpu.VMEM((PEERS, STATE + 16, width // PEERS), BF16),
+            pltpu.SemaphoreType.DMA((12,)),
         ),
         grant=None,
+        out=HBM,
     )(begin, doc, rate, dt, x, b, k, v)
     got = lax.all_to_all(own_states, "x", 0, 0, tiled=True)
 
@@ -321,6 +341,11 @@
         [VMEM] * 2,
         flops=10**6,
         moved=10**6,
+        scratch=(
+            pltpu.VMEM((PEERS, STATE, width // PEERS), BF16),
+            pltpu.SemaphoreType.DMA((PEERS,)),
+        ),
+        out=HBM,
     )(got, before)
     own, factor, gain = call(
         inside,

time: 57.6 us -> 57.1 us (level)
  the two profiles are of different devices: /device:TPU:64 before, /device:TPU:192 now
where the time goes in v3:
time: 57.1 us; the launch traced here: 56.7 us
  starting transfers between devices  20.7 us (36%)
  blocking collectives  14.7 us (26%)
  waiting for transfers between devices  10.7 us (19%)
  Pallas kernels  9.14 us (16%)
  between operations  0.84 us (1%)
  local copies, waits for them, and re-layouts  0.64 us (1%)
    all_to_all x1, blocking collectives, local(): lax.all_to_all(rows.reshape(tp, ROWS // tp, 2 * width), 'tp', 0, 0, tiled...  14.7 us
    ppermute x2, starting transfers between devices, along(): lax.ppermute(a, ('z', 'x'), [(i - distance, i) for i in range(distance, c...  6.69 us
    all_to_all x1, starting transfers between devices, local(): carried = lax.all_to_all(carried, 'x', 0, 0, tiled=True)  5.73 us
    ppermute x2, waiting for transfers between devices, along(): lax.ppermute(a, ('z', 'x'), [(i - distance, i) for i in range(distance, c...  4.78 us
    all_to_all x1, starting transfers between devices, local(): got = lax.all_to_all(own_states, 'x', 0, 0, tiled=True)  4.44 us
    ppermute x1, starting transfers between devices, local(): lax.ppermute(group, 'z', [(i - 1, i) for i in range(1, lax.axis_size('z'))])  3.83 us
    pallas_call x1, Pallas kernels, local(): call(attention, shaped((ROWS, width), BF16), [SMEM, SMEM] + [VMEM] * 5, f...  3.12 us
    all_to_all x1, waiting for transfers between devices, local(): carried = lax.all_to_all(carried, 'x', 0, 0, tiled=True)  2.81 us
  transfers between devices with their start and end apart: 5, of which 4 were waited for; matrix products, arithmetic and copies ran while one was open for 0% of the time, Pallas kernels for 10%

profile of v3, /device:TPU:192, one launch (start us, length us, event | category | flops | bytes accessed | tf_op | source)
XLA Modules:
  0.0 56.7 jit_solution(17877734800149259165)
XLA Ops:
  0.6 2.5 %shard_map.122 = (bf16[4,272,256]{2,1,0:T(8,128)(2,1)}, bf16[128,256]{1,0:T(8,128)(2,1)}) custom-call(s32[1]{0:T(128)} %bitcast.begin_ref, s32[32]{0:T(128)} %doc_ref.3, f32[16]{0:T(128)} %rate_ref.1, f32[16,128]{1,0:T(8,128)} %bitcast.5, bf16[128,1024]{1,0:T(8,128)(2,1)} %x_ref.1, bf16[128,256]{1,0:T(8,128)(2,1)} %b_ref.1, bf16[128,128]{1,0:T(8,128)(2,1)} %k_hbm.1, ...), custom_call_target="tpu_custom_call" | custom-call | flops 100000000 | bytes 1000000 | tf_op jit(solution)/shard_map/pallas_call | solution.py:302
  3.1 0.0 copy-start.4
  3.1 4.4 %all-to-all-start = ((bf16[4,272,256]{2,1,0:T(8,128)(2,1)}), bf16[4,272,256]{2,1,0:T(8,128)(2,1)S(1)}, u32[]{:S(2)}, u32[]{:S(2)}) async-start(bf16[4,272,256]{2,1,0:T(8,128)(2,1)} %get-tuple-element.7), calls=%async_computation | async-start | bytes 1114112 | tf_op jit(solution)/shard_map/all_to_all | solution.py:321
  7.6 0.0 copy-done.4
  7.6 3.9 %collective-permute-start = (bf16[128,256]{1,0:T(8,128)(2,1)S(1)}, bf16[128,256]{1,0:T(8,128)(2,1)S(1)}, u32[]{:S(2)}, u32[]{:S(2)}) collective-permute-start(bf16[128,256]{1,0:T(8,128)(2,1)S(1)} %copy-done.4), channel_id=1, source_target_pairs={{0,8},{8,16},{16,24},{24,32},{32,40},{40,48},{48,56},{56,64},{64,7... | collective-permute-start | bytes 196616 | tf_op jit(solution)/shard_map/ppermute | solution.py:325
  11.5 4.8 %collective-permute-done.near_ref.kv1_ref = bf16[128,256]{1,0:T(8,128)(2,1)S(1)} collective-permute-done((bf16[128,256]{1,0:T(8,128)(2,1)S(1)}, bf16[128,256]{1,0:T(8,128)(2,1)S(1)}, u32[]{:S(2)}, u32[]{:S(2)}) %collective-permute-start) | collective-permute-done | bytes 65568 | tf_op jit(solution)/shard_map/ppermute | solution.py:325
  16.3 2.2 %all-to-all-done.got_ref = bf16[4,272,256]{2,1,0:T(8,128)(2,1)S(1)} async-done(((bf16[4,272,256]{2,1,0:T(8,128)(2,1)}), bf16[4,272,256]{2,1,0:T(8,128)(2,1)S(1)}, u32[]{:S(2)}, u32[]{:S(2)}) %all-to-all-start) | async-done | bytes 557088 | tf_op jit(solution)/shard_map/all_to_all | solution.py:321
  18.5 0.1 shard_map.123
  18.6 3.8 %collective-permute-start.1 = (bf16[384,256]{1,0:T(8,128)(2,1)S(1)}, bf16[384,256]{1,0:T(8,128)(2,1)S(1)}, u32[]{:S(2)}, u32[]{:S(2)}) collective-permute-start(bf16[384,256]{1,0:T(8,128)(2,1)S(1)} %shard_map.123), channel_id=1, source_target_pairs={{0,32},{32,64},{64,96},{96,128},{128,160},{160,192},{192,224},{224... | collective-permute-start | bytes 589832 | tf_op jit(solution)/shard_map/ppermute | solution.py:337
  22.5 2.8 %collective-permute-start.2 = (bf16[256,256]{1,0:T(8,128)(2,1)S(1)}, bf16[256,256]{1,0:T(8,128)(2,1)S(1)}, u32[]{:S(2)}, u32[]{:S(2)}) collective-permute-start(bf16[256,256]{1,0:T(8,128)(2,1)S(1)} %shard_map.126), channel_id=1, source_target_pairs={{0,16},{8,24},{16,32},{24,40},{32,48},{40,56},{48,64},{56,72},{64,... | collective-permute-start | bytes 393224 | tf_op jit(solution)/shard_map/ppermute | solution.py:325
  25.2 0.9 %collective-permute-done.1.before_ref.kv4_ref = bf16[384,256]{1,0:T(8,128)(2,1)S(1)} collective-permute-done((bf16[384,256]{1,0:T(8,128)(2,1)S(1)}, bf16[384,256]{1,0:T(8,128)(2,1)S(1)}, u32[]{:S(2)}, u32[]{:S(2)}) %collective-permute-start.1) | collective-permute-done | bytes 196640 | tf_op jit(solution)/shard_map/ppermute | solution.py:337
  26.2 0.9 %shard_map.124.carried_ref = bf16[4,256,256]{2,1,0:T(8,128)(2,1)} custom-call(bf16[4,272,256]{2,1,0:T(8,128)(2,1)S(1)} %all-to-all-done.got_ref, bf16[384,256]{1,0:T(8,128)(2,1)S(1)} %collective-permute-done.1.before_ref.kv4_ref), custom_call_target="tpu_custom_call" | custom-call | flops 1000000 | bytes 1000000 | tf_op jit(solution)/shard_map/pallas_call | solution.py:338
  27.0 0.0 copy-start.7
  27.0 0.0 copy-start.9
  27.1 5.7 %all-to-all-start.1 = ((bf16[4,256,256]{2,1,0:T(8,128)(2,1)}), bf16[4,256,256]{2,1,0:T(8,128)(2,1)S(1)}, u32[]{:S(2)}, u32[]{:S(2)}) async-start(bf16[4,256,256]{2,1,0:T(8,128)(2,1)} %shard_map.124.carried_ref), calls=%async_computation.1 | async-start | bytes 1048576 | tf_op jit(solution)/shard_map/all_to_all | solution.py:358
  32.8 0.0 copy-start.3
  32.8 0.0 copy-start.5
  32.8 0.0 collective-permute-done.2.pair_ref
  32.8 0.0 copy-done.7
  32.8 0.0 copy-done.9
  32.9 0.0 copy-start.6
  32.9 3.1 %shard_map.127.att_ref = bf16[128,1024]{1,0:T(8,128)(2,1)S(1)} custom-call(s32[1]{0:T(128)} %bitcast.begin_ref, s32[32]{0:T(128)S(1)} %copy-done.7, bf16[128,1024]{1,0:T(8,128)(2,1)S(1)} %copy-done.9, bf16[128,256]{1,0:T(8,128)(2,1)S(1)} %copy-done.4, bf16[128,256]{1,0:T(8,128)(2,1)S(1)} %collective-permute-done.near_ref.kv1_ref, ...), custom_call_target="tpu_custom_call" | custom-call | flops 10000000000 | bytes 100000000 | tf_op jit(solution)/shard_map/pallas_call | solution.py:359
  36.0 0.0 copy-start.8
  36.0 0.0 copy-done
  36.0 0.0 copy-done.1
  36.0 0.0 copy-done.2
  36.1 0.6 %copy-done.8 = f32[16]{0:T(128)S(1)} copy-done((f32[16]{0:T(128)S(1)}, f32[16]{0:T(128)}, u32[]{:S(2)}) %copy-start.8) | copy-done | bytes 88
  36.7 1.4 %shard_map.125 = (f32[128,1024]{1,0:T(8,128)S(1)}, f32[128,1024]{1,0:T(8,128)S(1)}, f32[1,1024]{1,0:T(1,128)S(1)}) custom-call(s32[1]{0:T(128)} %bitcast.begin_ref, s32[32]{0:T(128)S(1)} %copy-done.7, f32[16]{0:T(128)S(1)} %copy-done.8, bf16[128,1024]{1,0:T(8,128)(2,1)S(1)} %copy-done, bf16[128,256]{1,0:T(8,128)(2,1)S(1)} %copy-done.2, ...), custom_call_target="tpu_custom_call" | custom-call | flops 100000000 | bytes 1000000 | tf_op jit(solution)/shard_map/pallas_call | solution.py:350
  38.1 2.8 %all-to-all-done.1.carried_ref = bf16[4,256,256]{2,1,0:T(8,128)(2,1)S(1)} async-done(((bf16[4,256,256]{2,1,0:T(8,128)(2,1)}), bf16[4,256,256]{2,1,0:T(8,128)(2,1)S(1)}, u32[]{:S(2)}, u32[]{:S(2)}) %all-to-all-start.1) | async-done | bytes 524320 | tf_op jit(solution)/shard_map/all_to_all | solution.py:358
  40.9 0.3 shard_map.128
  41.2 14.7 %all_to_all.15.got_ref = bf16[8,16,2048]{2,1,0:T(8,128)(2,1)S(1)} all-to-all(bf16[8,16,2048]{2,1,0:T(8,128)(2,1)S(1)} %bitcast.4), channel_id=1, replica_groups=mesh['z'=16,'x'=4,'tp'=8] {'tp'}, dimensions={0} | all-to-all | bytes 1048576 | tf_op jit(solution)/shard_map/all_to_all | solution.py:376
  55.9 0.8 %shard_map.129 = (bf16[16,8192]{1,0:T(8,128)(2,1)}, bf16[16,8192]{1,0:T(8,128)(2,1)}) custom-call(bf16[8,16,2048]{2,1,0:T(8,128)(2,1)S(1)} %all_to_all.15.got_ref), custom_call_target="tpu_custom_call" | custom-call | bytes 1000000 | tf_op jit(solution)/shard_map/pallas_call | solution.py:377
  (7 shorter events, 0.0 us)
Async XLA Ops:
  3.1 4.5 %copy-start.4 = (bf16[128,256]{1,0:T(8,128)(2,1)S(1)}, bf16[128,256]{1,0:T(8,128)(2,1)}, u32[]{:S(2)}) copy-start(bf16[128,256]{1,0:T(8,128)(2,1)} %get-tuple-element.8.kv_ref.kv0_ref) | copy-start | bytes 196612
  3.1 15.4 %all-to-all-start = ((bf16[4,272,256]{2,1,0:T(8,128)(2,1)}), bf16[4,272,256]{2,1,0:T(8,128)(2,1)S(1)}, u32[]{:S(2)}, u32[]{:S(2)}) async-start(bf16[4,272,256]{2,1,0:T(8,128)(2,1)} %get-tuple-element.7), calls=%async_computation | async-start | bytes 1114112 | tf_op jit(solution)/shard_map/all_to_all | solution.py:321
  7.6 8.7 %collective-permute-start = (bf16[128,256]{1,0:T(8,128)(2,1)S(1)}, bf16[128,256]{1,0:T(8,128)(2,1)S(1)}, u32[]{:S(2)}, u32[]{:S(2)}) collective-permute-start(bf16[128,256]{1,0:T(8,128)(2,1)S(1)} %copy-done.4), channel_id=1, source_target_pairs={{0,8},{8,16},{16,24},{24,32},{32,40},{40,48},{48,56},{56,64},{64,7... | collective-permute-start | bytes 196616 | tf_op jit(solution)/shard_map/ppermute | solution.py:325
  18.6 7.6 %collective-permute-start.1 = (bf16[384,256]{1,0:T(8,128)(2,1)S(1)}, bf16[384,256]{1,0:T(8,128)(2,1)S(1)}, u32[]{:S(2)}, u32[]{:S(2)}) collective-permute-start(bf16[384,256]{1,0:T(8,128)(2,1)S(1)} %shard_map.123), channel_id=1, source_target_pairs={{0,32},{32,64},{64,96},{96,128},{128,160},{160,192},{192,224},{224... | collective-permute-start | bytes 589832 | tf_op jit(solution)/shard_map/ppermute | solution.py:337
  22.5 10.4 %collective-permute-start.2 = (bf16[256,256]{1,0:T(8,128)(2,1)S(1)}, bf16[256,256]{1,0:T(8,128)(2,1)S(1)}, u32[]{:S(2)}, u32[]{:S(2)}) collective-permute-start(bf16[256,256]{1,0:T(8,128)(2,1)S(1)} %shard_map.126), channel_id=1, source_target_pairs={{0,16},{8,24},{16,32},{24,40},{32,48},{40,56},{48,64},{56,72},{64,... | collective-permute-start | bytes 393224 | tf_op jit(solution)/shard_map/ppermute | solution.py:325
  27.0 5.8 %copy-start.7 = (s32[32]{0:T(128)S(1)}, s32[32]{0:T(128)}, u32[]{:S(2)}) copy-start(s32[32]{0:T(128)} %doc_ref.3) | copy-start | bytes 388
  27.0 5.8 %copy-start.9 = (bf16[128,1024]{1,0:T(8,128)(2,1)S(1)}, bf16[128,1024]{1,0:T(8,128)(2,1)}, u32[]{:S(2)}) copy-start(bf16[128,1024]{1,0:T(8,128)(2,1)} %q_ref.1) | copy-start | bytes 786436
  27.1 13.8 %all-to-all-start.1 = ((bf16[4,256,256]{2,1,0:T(8,128)(2,1)}), bf16[4,256,256]{2,1,0:T(8,128)(2,1)S(1)}, u32[]{:S(2)}, u32[]{:S(2)}) async-start(bf16[4,256,256]{2,1,0:T(8,128)(2,1)} %shard_map.124.carried_ref), calls=%async_computation.1 | async-start | bytes 1048576 | tf_op jit(solution)/shard_map/all_to_all | solution.py:358
  32.8 3.2 %copy-start = (bf16[128,1024]{1,0:T(8,128)(2,1)S(1)}, bf16[128,1024]{1,0:T(8,128)(2,1)}, u32[]{:S(2)}) copy-start(bf16[128,1024]{1,0:T(8,128)(2,1)} %x_ref.1) | copy-start | bytes 786436
  32.8 3.2 %copy-start.1 = (bf16[128,1024]{1,0:T(8,128)(2,1)S(1)}, bf16[128,1024]{1,0:T(8,128)(2,1)}, u32[]{:S(2)}) copy-start(bf16[128,1024]{1,0:T(8,128)(2,1)} %gate_ref.1) | copy-start | bytes 786436
  32.8 3.2 %copy-start.2 = (bf16[128,256]{1,0:T(8,128)(2,1)S(1)}, bf16[128,256]{1,0:T(8,128)(2,1)}, u32[]{:S(2)}) copy-start(bf16[128,256]{1,0:T(8,128)(2,1)} %b_ref.1) | copy-start | bytes 196612
  32.8 3.2 %copy-start.3 = (bf16[128,256]{1,0:T(8,128)(2,1)S(1)}, bf16[128,256]{1,0:T(8,128)(2,1)}, u32[]{:S(2)}) copy-start(bf16[128,256]{1,0:T(8,128)(2,1)} %c_ref.3) | copy-start | bytes 196612
  32.8 3.2 %copy-start.5 = (f32[128,16]{0,1:T(8,128)S(1)}, f32[128,16]{0,1:T(8,128)}, u32[]{:S(2)}) copy-start(f32[128,16]{0,1:T(8,128)} %param.16) | copy-start | bytes 24580
  32.9 3.2 %copy-start.6 = (f32[1024]{0:T(1024)S(1)}, f32[1024]{0:T(1024)}, u32[]{:S(2)}) copy-start(f32[1024]{0:T(1024)} %param.18) | copy-start | bytes 12292
  36.0 0.7 %copy-start.8 = (f32[16]{0:T(128)S(1)}, f32[16]{0:T(128)}, u32[]{:S(2)}) copy-start(f32[16]{0:T(128)} %rate_ref.1) | copy-start | bytes 196

commit v4 on v3

--- a/solution.py
+++ b/solution.py
@@ -171,8 +171,8 @@
     pair_ref[ROWS:, :] = near_ref[...]
 
 
-def group_state(got_ref, kv_ref, near_ref, out_ref):
-    del near_ref
+def group_state(got_ref, kv_ref, near_ref, own_ref, out_ref):
+    del near_ref, own_ref
     total, _ = received(got_ref, 0)
     for j in range(1, PEERS):
         state, transmit = received(got_ref, j)
@@ -182,15 +182,17 @@
 
 
 def carried_states(got_ref, before_ref, out_hbm, out_ref, sems):
+    copies = [
+        pltpu.make_async_copy(out_ref.at[j], out_hbm.at[j], sems.at[j]) for j in range(PEERS)
+    ]
+    out_ref[0] = before_ref[:STATE, :]
+    copies[0].start()
     carried = before_ref[:STATE, :].astype(F32)
-    copies = []
-    for j in range(PEERS):
+    for j in range(1, PEERS):
+        state, transmit = received(got_ref, j - 1)
+        carried = carried * transmit + state
         out_ref[j] = carried.astype(BF16)
-        copies.append(pltpu.make_async_copy(out_ref.at[j], out_hbm.at[j], sems.at[j]))
         copies[j].start()
-        if j < PEERS - 1:
-            state, transmit = received(got_ref, j)
-            carried = carried * transmit + state
     for copy in copies:
         copy.wait()
 
@@ -210,12 +212,10 @@
     dt_ref,
     gate_ref,
     gain_ref,
-    carried_ref,
     own_ref,
     factor_ref,
     gain_out_ref,
 ):
-    del carried_ref
     begin = begin_ref[0]
     gain_out_ref[...] = gain_ref[...]
     starts = start_columns(doc_ref, begin)
@@ -246,12 +246,12 @@
         factor_ref[:, at] = entry * gate
 
 
-def attention(begin_ref, doc_ref, q_ref, kv0_ref, kv1_ref, pair_ref, kv4_ref, out_ref):
+def attention(begin_ref, doc_ref, q_ref, kv0_ref, kv2_ref, pair_ref, kv4_ref, out_ref):
     begin = begin_ref[0]
     starts = start_columns(doc_ref, begin)
     row = lax.broadcasted_iota(jnp.int32, (ROWS, ROWS), 0)
     lane = lax.broadcasted_iota(jnp.int32, (ROWS, ROWS), 1)
-    blocks = [kv0_ref[...], kv1_ref[...], pair_ref[:ROWS, :], pair_ref[ROWS:, :], kv4_ref[STATE:, :]]
+    blocks = [kv0_ref[...], pair_ref[:ROWS, :], kv2_ref[...], pair_ref[ROWS:, :], kv4_ref[STATE:, :]]
     bias = []
     for j in range(len(blocks)):
         allowed = (begin - j * ROWS + lane).astype(F32) >= starts
@@ -324,16 +324,24 @@
         count = lax.axis_size("z") * PEERS
         return lax.ppermute(a, ("z", "x"), [(i - distance, i) for i in range(distance, count)])
 
-    kv1 = along(kv, 1)
-    pair = call(pair_up, shaped((2 * ROWS, 2 * ROWS), BF16), [VMEM] * 2, moved=10**8)(kv, kv1)
-    pair = along(pair, 2)
+    kv2 = along(kv, 2)
+    pair = call(pair_up, shaped((2 * ROWS, 2 * ROWS), BF16), [VMEM] * 2, moved=10**8)(kv, kv2)
+    pair = along(pair, 1)
+    own, factor, gain = call(
+        inside,
+        (shaped((ROWS, width), F32), shaped((ROWS, width), F32), shaped((1, width), F32)),
+        [SMEM, SMEM, SMEM] + [VMEM] * 6,
+        flops=10**8,
+        moved=10**6,
+        exps=400000,
+    )(begin, doc, rate, x, b, c, dt, gate, weight.reshape(1, width))
     group = call(
         group_state,
         shaped((STATE + ROWS, width // PEERS), BF16),
-        [VMEM] * 2 + [LATER],
+        [VMEM] * 2 + [LATER] * 2,
         flops=10**6,
         moved=10**6,
-    )(got, kv, kv1)
+    )(got, kv, kv2, own)
     before = lax.ppermute(group, "z", [(i - 1, i) for i in range(1, lax.axis_size("z"))])
     carried = call(
         carried_states,
@@ -347,14 +355,6 @@
         ),
         out=HBM,
     )(got, before)
-    own, factor, gain = call(
-        inside,
-        (shaped((ROWS, width), F32), shaped((ROWS, width), F32), shaped((1, width), F32)),
-        [SMEM, SMEM, SMEM] + [VMEM] * 6 + [LATER],
-        flops=10**8,
-        moved=10**6,
-        exps=400000,
-    )(begin, doc, rate, x, b, c, dt, gate, weight.reshape(1, width), carried)
     carried = lax.all_to_all(carried, "x", 0, 0, tiled=True)
     att = call(
         attention,
@@ -363,7 +363,7 @@
         flops=10**10,
         moved=10**8,
         exps=10**8,
-    )(begin, doc, q, kv, kv1, pair, before)
+    )(begin, doc, q, kv, kv2, pair, before)
     rows = pl.pallas_call(
         finish,
         out_shape=shaped((ROWS, 2 * width), BF16),

time: 57.1 us -> 57.1 us (level)
  starting transfers between devices: 20.7 us -> 21.7 us
  local copies, waits for them, and re-layouts: 0.64 us -> 0.06 us
    ppermute x2, waiting for transfers between devices: 4.78 us -> 1.78 us  [along(): lax.ppermute(a, ('z', 'x'), [(i - distance, i) for i in range(distance, c...]
    all_to_all x1, waiting for transfers between devices: 2.81 us -> 4.84 us  [local(): carried = lax.all_to_all(carried, 'x', 0, 0, tiled=True)]
    ppermute x2, starting transfers between devices: 6.69 us -> 8.03 us  [along(): lax.ppermute(a, ('z', 'x'), [(i - distance, i) for i in range(distance, c...]
    unnamed x20, local copies, waits for them, and re-layouts: 0.64 us -> 0.06 us
where the time goes in v4:
time: 57.1 us; the launch traced here: 56.8 us
  starting transfers between devices  21.7 us (38%)
  blocking collectives  14.7 us (26%)
  waiting for transfers between devices  10.2 us (18%)
  Pallas kernels  9.27 us (16%)
  between operations  0.84 us (1%)
    all_to_all x1, blocking collectives, local(): lax.all_to_all(rows.reshape(tp, ROWS // tp, 2 * width), 'tp', 0, 0, tiled...  14.7 us
    ppermute x2, starting transfers between devices, along(): lax.ppermute(a, ('z', 'x'), [(i - distance, i) for i in range(distance, c...  8.03 us
    all_to_all x1, starting transfers between devices, local(): carried = lax.all_to_all(carried, 'x', 0, 0, tiled=True)  5.44 us
    all_to_all x1, waiting for transfers between devices, local(): carried = lax.all_to_all(carried, 'x', 0, 0, tiled=True)  4.84 us
    all_to_all x1, starting transfers between devices, local(): got = lax.all_to_all(own_states, 'x', 0, 0, tiled=True)  4.44 us
    ppermute x1, starting transfers between devices, local(): lax.ppermute(group, 'z', [(i - 1, i) for i in range(1, lax.axis_size('z'))])  3.83 us
    pallas_call x1, Pallas kernels, local(): call(attention, shaped((ROWS, width), BF16), [SMEM, SMEM] + [VMEM] * 5, f...  3.22 us
    pallas_call x1, Pallas kernels, local(): call(prepare, (shaped((PEERS, STATE + 16, width // PEERS), BF16), shaped(...  2.48 us
  transfers between devices with their start and end apart: 5, of which 4 were waited for; matrix products, arithmetic and copies ran while one was open for 0% of the time, Pallas kernels for 10%

profile of v4, /device:TPU:192, one launch (start us, length us, event | category | flops | bytes accessed | tf_op | source)
XLA Modules:
  0.0 56.8 jit_solution(6176248972572975804)
XLA Ops:
  0.6 2.5 %shard_map.122 = (bf16[4,272,256]{2,1,0:T(8,128)(2,1)}, bf16[128,256]{1,0:T(8,128)(2,1)}) custom-call(s32[1]{0:T(128)} %bitcast.begin_ref, s32[32]{0:T(128)} %doc_ref.3, f32[16]{0:T(128)} %rate_ref.1, f32[16,128]{1,0:T(8,128)} %bitcast.5, bf16[128,1024]{1,0:T(8,128)(2,1)} %x_ref.1, bf16[128,256]{1,0:T(8,128)(2,1)} %b_ref.1, bf16[128,128]{1,0:T(8,128)(2,1)} %k_hbm.1, ...), custom_call_target="tpu_custom_call" | custom-call | flops 100000000 | bytes 1000000 | tf_op jit(solution)/shard_map/pallas_call | solution.py:302
  3.1 0.0 copy-start.1
  3.1 0.0 copy-start
  3.1 0.0 copy-start.2
  3.2 0.0 copy-start.3
  3.2 0.0 copy-start.4
  3.2 0.0 copy-start.7
  3.2 0.0 copy-start.9
  3.2 4.4 %all-to-all-start = ((bf16[4,272,256]{2,1,0:T(8,128)(2,1)}), bf16[4,272,256]{2,1,0:T(8,128)(2,1)S(1)}, u32[]{:S(2)}, u32[]{:S(2)}) async-start(bf16[4,272,256]{2,1,0:T(8,128)(2,1)} %get-tuple-element.7), calls=%async_computation | async-start | bytes 1114112 | tf_op jit(solution)/shard_map/all_to_all | solution.py:321
  7.6 0.0 copy-done.1
  7.7 5.6 %collective-permute-start = (bf16[128,256]{1,0:T(8,128)(2,1)S(1)}, bf16[128,256]{1,0:T(8,128)(2,1)S(1)}, u32[]{:S(2)}, u32[]{:S(2)}) collective-permute-start(bf16[128,256]{1,0:T(8,128)(2,1)S(1)} %copy-done.1), channel_id=1, source_target_pairs={{0,16},{8,24},{16,32},{24,40},{32,48},{40,56},{48,64},{56,72},{64,... | collective-permute-start | bytes 196616 | tf_op jit(solution)/shard_map/ppermute | solution.py:325
  13.2 0.0 copy-done
  13.2 0.0 copy-done.2
  13.2 0.0 copy-done.3
  13.3 0.0 copy-done.4
  13.3 1.4 %shard_map.123 = (f32[128,1024]{1,0:T(8,128)S(1)}, f32[128,1024]{1,0:T(8,128)S(1)}, f32[1,1024]{1,0:T(1,128)S(1)}) custom-call(s32[1]{0:T(128)} %bitcast.begin_ref, s32[32]{0:T(128)S(1)} %copy-done.6, f32[16]{0:T(128)S(1)} %copy-done.5, bf16[128,1024]{1,0:T(8,128)(2,1)S(1)} %copy-done, bf16[128,256]{1,0:T(8,128)(2,1)S(1)} %copy-done.2, ...), custom_call_target="tpu_custom_call" | custom-call | flops 100000000 | bytes 1000000 | tf_op jit(solution)/shard_map/pallas_call | solution.py:330
  14.7 1.8 %collective-permute-done.near_ref.kv2_ref = bf16[128,256]{1,0:T(8,128)(2,1)S(1)} collective-permute-done((bf16[128,256]{1,0:T(8,128)(2,1)S(1)}, bf16[128,256]{1,0:T(8,128)(2,1)S(1)}, u32[]{:S(2)}, u32[]{:S(2)}) %collective-permute-start) | collective-permute-done | bytes 65568 | tf_op jit(solution)/shard_map/ppermute | solution.py:325
  16.5 2.4 %all-to-all-done.got_ref = bf16[4,272,256]{2,1,0:T(8,128)(2,1)S(1)} async-done(((bf16[4,272,256]{2,1,0:T(8,128)(2,1)}), bf16[4,272,256]{2,1,0:T(8,128)(2,1)S(1)}, u32[]{:S(2)}, u32[]{:S(2)}) %all-to-all-start) | async-done | bytes 557088 | tf_op jit(solution)/shard_map/all_to_all | solution.py:321
  18.9 0.1 shard_map.124
  19.0 3.8 %collective-permute-start.1 = (bf16[384,256]{1,0:T(8,128)(2,1)S(1)}, bf16[384,256]{1,0:T(8,128)(2,1)S(1)}, u32[]{:S(2)}, u32[]{:S(2)}) collective-permute-start(bf16[384,256]{1,0:T(8,128)(2,1)S(1)} %shard_map.124), channel_id=1, source_target_pairs={{0,32},{32,64},{64,96},{96,128},{128,160},{160,192},{192,224},{224... | collective-permute-start | bytes 589832 | tf_op jit(solution)/shard_map/ppermute | solution.py:345
  22.8 2.5 %collective-permute-start.2 = (bf16[256,256]{1,0:T(8,128)(2,1)S(1)}, bf16[256,256]{1,0:T(8,128)(2,1)S(1)}, u32[]{:S(2)}, u32[]{:S(2)}) collective-permute-start(bf16[256,256]{1,0:T(8,128)(2,1)S(1)} %shard_map.126), channel_id=1, source_target_pairs={{0,8},{8,16},{16,24},{24,32},{32,40},{40,48},{48,56},{56,64},{64,7... | collective-permute-start | bytes 393224 | tf_op jit(solution)/shard_map/ppermute | solution.py:325
  25.3 1.2 %collective-permute-done.1.before_ref.kv4_ref = bf16[384,256]{1,0:T(8,128)(2,1)S(1)} collective-permute-done((bf16[384,256]{1,0:T(8,128)(2,1)S(1)}, bf16[384,256]{1,0:T(8,128)(2,1)S(1)}, u32[]{:S(2)}, u32[]{:S(2)}) %collective-permute-start.1) | collective-permute-done | bytes 196640 | tf_op jit(solution)/shard_map/ppermute | solution.py:345
  26.5 0.9 %shard_map.125 = bf16[4,256,256]{2,1,0:T(8,128)(2,1)} custom-call(bf16[4,272,256]{2,1,0:T(8,128)(2,1)S(1)} %all-to-all-done.got_ref, bf16[384,256]{1,0:T(8,128)(2,1)S(1)} %collective-permute-done.1.before_ref.kv4_ref), custom_call_target="tpu_custom_call" | custom-call | flops 1000000 | bytes 1000000 | tf_op jit(solution)/shard_map/pallas_call | solution.py:346
  27.4 0.0 copy-start.8
  27.4 5.4 %all-to-all-start.1 = ((bf16[4,256,256]{2,1,0:T(8,128)(2,1)}), bf16[4,256,256]{2,1,0:T(8,128)(2,1)S(1)}, u32[]{:S(2)}, u32[]{:S(2)}) async-start(bf16[4,256,256]{2,1,0:T(8,128)(2,1)} %shard_map.125), calls=%async_computation.1 | async-start | bytes 1048576 | tf_op jit(solution)/shard_map/all_to_all | solution.py:358
  32.9 0.0 collective-permute-done.2.pair_ref
  32.9 0.0 copy-done.8
  32.9 3.2 %shard_map.127.att_ref = bf16[128,1024]{1,0:T(8,128)(2,1)S(1)} custom-call(s32[1]{0:T(128)} %bitcast.begin_ref, s32[32]{0:T(128)S(1)} %copy-done.6, bf16[128,1024]{1,0:T(8,128)(2,1)S(1)} %copy-done.8, bf16[128,256]{1,0:T(8,128)(2,1)S(1)} %copy-done.1, bf16[128,256]{1,0:T(8,128)(2,1)S(1)} %collective-permute-done.near_ref.kv2_ref, ...), custom_call_target="tpu_custom_call" | custom-call | flops 10000000000 | bytes 100000000 | tf_op jit(solution)/shard_map/pallas_call | solution.py:359
  36.1 4.8 %all-to-all-done.1.carried_ref = bf16[4,256,256]{2,1,0:T(8,128)(2,1)S(1)} async-done(((bf16[4,256,256]{2,1,0:T(8,128)(2,1)}), bf16[4,256,256]{2,1,0:T(8,128)(2,1)S(1)}, u32[]{:S(2)}, u32[]{:S(2)}) %all-to-all-start.1) | async-done | bytes 524320 | tf_op jit(solution)/shard_map/all_to_all | solution.py:358
  40.9 0.4 shard_map.128
  41.3 14.7 %all_to_all.15.got_ref = bf16[8,16,2048]{2,1,0:T(8,128)(2,1)S(1)} all-to-all(bf16[8,16,2048]{2,1,0:T(8,128)(2,1)S(1)} %bitcast.4), channel_id=1, replica_groups=mesh['z'=16,'x'=4,'tp'=8] {'tp'}, dimensions={0} | all-to-all | bytes 1048576 | tf_op jit(solution)/shard_map/all_to_all | solution.py:376
  56.0 0.8 %shard_map.129 = (bf16[16,8192]{1,0:T(8,128)(2,1)}, bf16[16,8192]{1,0:T(8,128)(2,1)}) custom-call(bf16[8,16,2048]{2,1,0:T(8,128)(2,1)S(1)} %all_to_all.15.got_ref), custom_call_target="tpu_custom_call" | custom-call | bytes 1000000 | tf_op jit(solution)/shard_map/pallas_call | solution.py:377
  (7 shorter events, 0.0 us)
Async XLA Ops:
  3.1 4.5 %copy-start.1 = (bf16[128,256]{1,0:T(8,128)(2,1)S(1)}, bf16[128,256]{1,0:T(8,128)(2,1)}, u32[]{:S(2)}) copy-start(bf16[128,256]{1,0:T(8,128)(2,1)} %get-tuple-element.8.kv_ref.kv0_ref) | copy-start | bytes 196612
  3.1 10.1 %copy-start = (bf16[128,1024]{1,0:T(8,128)(2,1)S(1)}, bf16[128,1024]{1,0:T(8,128)(2,1)}, u32[]{:S(2)}) copy-start(bf16[128,1024]{1,0:T(8,128)(2,1)} %x_ref.1) | copy-start | bytes 786436
  3.1 10.1 %copy-start.2 = (bf16[128,256]{1,0:T(8,128)(2,1)S(1)}, bf16[128,256]{1,0:T(8,128)(2,1)}, u32[]{:S(2)}) copy-start(bf16[128,256]{1,0:T(8,128)(2,1)} %b_ref.1) | copy-start | bytes 196612
  3.2 10.1 %copy-start.3 = (bf16[128,256]{1,0:T(8,128)(2,1)S(1)}, bf16[128,256]{1,0:T(8,128)(2,1)}, u32[]{:S(2)}) copy-start(bf16[128,256]{1,0:T(8,128)(2,1)} %c_ref.3) | copy-start | bytes 196612
  3.2 10.1 %copy-start.4 = (f32[128,16]{0,1:T(8,128)S(1)}, f32[128,16]{0,1:T(8,128)}, u32[]{:S(2)}) copy-start(f32[128,16]{0,1:T(8,128)} %param.16) | copy-start | bytes 24580
  3.2 10.1 %copy-start.7 = (bf16[128,1024]{1,0:T(8,128)(2,1)S(1)}, bf16[128,1024]{1,0:T(8,128)(2,1)}, u32[]{:S(2)}) copy-start(bf16[128,1024]{1,0:T(8,128)(2,1)} %gate_ref.1) | copy-start | bytes 786436
  3.2 10.1 %copy-start.9 = (f32[1024]{0:T(1024)S(1)}, f32[1024]{0:T(1024)}, u32[]{:S(2)}) copy-start(f32[1024]{0:T(1024)} %param.18) | copy-start | bytes 12292
  3.2 15.7 %all-to-all-start = ((bf16[4,272,256]{2,1,0:T(8,128)(2,1)}), bf16[4,272,256]{2,1,0:T(8,128)(2,1)S(1)}, u32[]{:S(2)}, u32[]{:S(2)}) async-start(bf16[4,272,256]{2,1,0:T(8,128)(2,1)} %get-tuple-element.7), calls=%async_computation | async-start | bytes 1114112 | tf_op jit(solution)/shard_map/all_to_all | solution.py:321
  7.6 5.6 %copy-start.5 = (f32[16]{0:T(128)S(1)}, f32[16]{0:T(128)}, u32[]{:S(2)}) copy-start(f32[16]{0:T(128)} %rate_ref.1) | copy-start | bytes 196
  7.7 5.6 %copy-start.6 = (s32[32]{0:T(128)S(1)}, s32[32]{0:T(128)}, u32[]{:S(2)}) copy-start(s32[32]{0:T(128)} %doc_ref.3) | copy-start | bytes 388
  7.7 8.9 %collective-permute-start = (bf16[128,256]{1,0:T(8,128)(2,1)S(1)}, bf16[128,256]{1,0:T(8,128)(2,1)S(1)}, u32[]{:S(2)}, u32[]{:S(2)}) collective-permute-start(bf16[128,256]{1,0:T(8,128)(2,1)S(1)} %copy-done.1), channel_id=1, source_target_pairs={{0,16},{8,24},{16,32},{24,40},{32,48},{40,56},{48,64},{56,72},{64,... | collective-permute-start | bytes 196616 | tf_op jit(solution)/shard_map/ppermute | solution.py:325
  19.0 7.6 %collective-permute-start.1 = (bf16[384,256]{1,0:T(8,128)(2,1)S(1)}, bf16[384,256]{1,0:T(8,128)(2,1)S(1)}, u32[]{:S(2)}, u32[]{:S(2)}) collective-permute-start(bf16[384,256]{1,0:T(8,128)(2,1)S(1)} %shard_map.124), channel_id=1, source_target_pairs={{0,32},{32,64},{64,96},{96,128},{128,160},{160,192},{192,224},{224... | collective-permute-start | bytes 589832 | tf_op jit(solution)/shard_map/ppermute | solution.py:345
  22.8 10.0 %collective-permute-start.2 = (bf16[256,256]{1,0:T(8,128)(2,1)S(1)}, bf16[256,256]{1,0:T(8,128)(2,1)S(1)}, u32[]{:S(2)}, u32[]{:S(2)}) collective-permute-start(bf16[256,256]{1,0:T(8,128)(2,1)S(1)} %shard_map.126), channel_id=1, source_target_pairs={{0,8},{8,16},{16,24},{24,32},{32,40},{40,48},{48,56},{56,64},{64,7... | collective-permute-start | bytes 393224 | tf_op jit(solution)/shard_map/ppermute | solution.py:325
  27.4 5.5 %copy-start.8 = (bf16[128,1024]{1,0:T(8,128)(2,1)S(1)}, bf16[128,1024]{1,0:T(8,128)(2,1)}, u32[]{:S(2)}) copy-start(bf16[128,1024]{1,0:T(8,128)(2,1)} %q_ref.1) | copy-start | bytes 786436
  27.4 13.5 %all-to-all-start.1 = ((bf16[4,256,256]{2,1,0:T(8,128)(2,1)}), bf16[4,256,256]{2,1,0:T(8,128)(2,1)S(1)}, u32[]{:S(2)}, u32[]{:S(2)}) async-start(bf16[4,256,256]{2,1,0:T(8,128)(2,1)} %shard_map.125), calls=%async_computation.1 | async-start | bytes 1048576 | tf_op jit(solution)/shard_map/all_to_all | solution.py:358

commit v5 on v4

--- a/solution.py
+++ b/solution.py
@@ -181,17 +181,26 @@
     out_ref[STATE:, :] = kv_ref[...]
 
 
-def carried_states(got_ref, before_ref, out_hbm, out_ref, sems):
+def own_parts(got_ref, group_ref, part_ref, factor_ref):
+    del group_ref
+    part, factor = received(got_ref, 0)
+    for j in range(1, PEERS):
+        part_ref[j - 1] = part
+        factor_ref[j - 1] = jnp.broadcast_to(factor, factor_ref.shape[1:])
+        if j < PEERS - 1:
+            state, transmit = received(got_ref, j)
+            part, factor = part * transmit + state, factor * transmit
+
+
+def carried_states(part_ref, factor_ref, before_ref, out_hbm, out_ref, sems):
     copies = [
         pltpu.make_async_copy(out_ref.at[j], out_hbm.at[j], sems.at[j]) for j in range(PEERS)
     ]
     out_ref[0] = before_ref[:STATE, :]
     copies[0].start()
-    carried = before_ref[:STATE, :].astype(F32)
+    before = before_ref[:STATE, :].astype(F32)
     for j in range(1, PEERS):
-        state, transmit = received(got_ref, j - 1)
-        carried = carried * transmit + state
-        out_ref[j] = carried.astype(BF16)
+        out_ref[j] = (before * factor_ref[j - 1, :1] + part_ref[j - 1]).astype(BF16)
         copies[j].start()
     for copy in copies:
         copy.wait()
@@ -343,10 +352,20 @@
         moved=10**6,
     )(got, kv, kv2, own)
     before = lax.ppermute(group, "z", [(i - 1, i) for i in range(1, lax.axis_size("z"))])
+    part, factors = call(
+        own_parts,
+        (
+            shaped((PEERS - 1, STATE, width // PEERS), F32),
+            shaped((PEERS - 1, 8, width // PEERS), F32),
+        ),
+        [VMEM, LATER],
+        flops=10**6,
+        moved=10**6,
+    )(got, group)
     carried = call(
         carried_states,
         shaped((PEERS, STATE, width // PEERS), BF16),
-        [VMEM] * 2,
+        [VMEM] * 3,
         flops=10**6,
         moved=10**6,
         scratch=(
@@ -354,7 +373,7 @@
             pltpu.SemaphoreType.DMA((PEERS,)),
         ),
         out=HBM,
-    )(got, before)
+    )(part, factors, before)
     carried = lax.all_to_all(carried, "x", 0, 0, tiled=True)
     att = call(
         attention,

time: 57.1 us -> 57.2 us (level)
  no operation moved by 1% of the time
where the time goes in v5:
time: 57.2 us; the launch traced here: 56.9 us
  starting transfers between devices  21.8 us (38%)
  blocking collectives  14.7 us (26%)
  waiting for transfers between devices  10.1 us (18%)
  Pallas kernels  9.33 us (16%)
  between operations  0.85 us (1%)
    all_to_all x1, blocking collectives, local(): lax.all_to_all(rows.reshape(tp, ROWS // tp, 2 * width), 'tp', 0, 0, tiled...  14.7 us
    ppermute x2, starting transfers between devices, along(): lax.ppermute(a, ('z', 'x'), [(i - distance, i) for i in range(distance, c...  8.03 us
    all_to_all x1, starting transfers between devices, local(): carried = lax.all_to_all(carried, 'x', 0, 0, tiled=True)  5.53 us
    all_to_all x1, waiting for transfers between devices, local(): carried = lax.all_to_all(carried, 'x', 0, 0, tiled=True)  4.86 us
    all_to_all x1, starting transfers between devices, local(): got = lax.all_to_all(own_states, 'x', 0, 0, tiled=True)  4.44 us
    ppermute x1, starting transfers between devices, local(): lax.ppermute(group, 'z', [(i - 1, i) for i in range(1, lax.axis_size('z'))])  3.83 us
    pallas_call x1, Pallas kernels, local(): call(attention, shaped((ROWS, width), BF16), [SMEM, SMEM] + [VMEM] * 5, f...  3.2 us
    pallas_call x1, Pallas kernels, local(): call(prepare, (shaped((PEERS, STATE + 16, width // PEERS), BF16), shaped(...  2.48 us
  transfers between devices with their start and end apart: 5, of which 4 were waited for; matrix products, arithmetic and copies ran while one was open for 0% of the time, Pallas kernels for 10%

profile of v5, /device:TPU:192, one launch (start us, length us, event | category | flops | bytes accessed | tf_op | source)
XLA Modules:
  0.0 56.9 jit_solution(10878159068872545057)
XLA Ops:
  0.6 2.5 %shard_map.122 = (bf16[4,272,256]{2,1,0:T(8,128)(2,1)}, bf16[128,256]{1,0:T(8,128)(2,1)}) custom-call(s32[1]{0:T(128)} %bitcast.begin_ref, s32[32]{0:T(128)} %doc_ref.3, f32[16]{0:T(128)} %rate_ref.1, f32[16,128]{1,0:T(8,128)} %bitcast.5, bf16[128,1024]{1,0:T(8,128)(2,1)} %x_ref.1, bf16[128,256]{1,0:T(8,128)(2,1)} %b_ref.1, bf16[128,128]{1,0:T(8,128)(2,1)} %k_hbm.1, ...), custom_call_target="tpu_custom_call" | custom-call | flops 100000000 | bytes 1000000 | tf_op jit(solution)/shard_map/pallas_call | solution.py:311
  3.1 0.0 copy-start.1
  3.1 0.0 copy-start
  3.1 0.0 copy-start.2
  3.2 0.0 copy-start.3
  3.2 0.0 copy-start.4
  3.2 0.0 copy-start.7
  3.2 0.0 copy-start.9
  3.2 4.4 %all-to-all-start = ((bf16[4,272,256]{2,1,0:T(8,128)(2,1)}), bf16[4,272,256]{2,1,0:T(8,128)(2,1)S(1)}, u32[]{:S(2)}, u32[]{:S(2)}) async-start(bf16[4,272,256]{2,1,0:T(8,128)(2,1)} %get-tuple-element.9), calls=%async_computation | async-start | bytes 1114112 | tf_op jit(solution)/shard_map/all_to_all | solution.py:330
  7.6 0.0 copy-done.1
  7.7 5.6 %collective-permute-start = (bf16[128,256]{1,0:T(8,128)(2,1)S(1)}, bf16[128,256]{1,0:T(8,128)(2,1)S(1)}, u32[]{:S(2)}, u32[]{:S(2)}) collective-permute-start(bf16[128,256]{1,0:T(8,128)(2,1)S(1)} %copy-done.1), channel_id=1, source_target_pairs={{0,16},{8,24},{16,32},{24,40},{32,48},{40,56},{48,64},{56,72},{64,... | collective-permute-start | bytes 196616 | tf_op jit(solution)/shard_map/ppermute | solution.py:334
  13.2 0.0 copy-done
  13.2 0.0 copy-done.2
  13.2 0.0 copy-done.3
  13.3 0.0 copy-done.4
  13.3 1.4 %shard_map.123 = (f32[128,1024]{1,0:T(8,128)S(1)}, f32[128,1024]{1,0:T(8,128)S(1)}, f32[1,1024]{1,0:T(1,128)S(1)}) custom-call(s32[1]{0:T(128)} %bitcast.begin_ref, s32[32]{0:T(128)S(1)} %copy-done.6, f32[16]{0:T(128)S(1)} %copy-done.5, bf16[128,1024]{1,0:T(8,128)(2,1)S(1)} %copy-done, bf16[128,256]{1,0:T(8,128)(2,1)S(1)} %copy-done.2, ...), custom_call_target="tpu_custom_call" | custom-call | flops 100000000 | bytes 1000000 | tf_op jit(solution)/shard_map/pallas_call | solution.py:339
  14.7 1.8 %collective-permute-done.near_ref.kv2_ref = bf16[128,256]{1,0:T(8,128)(2,1)S(1)} collective-permute-done((bf16[128,256]{1,0:T(8,128)(2,1)S(1)}, bf16[128,256]{1,0:T(8,128)(2,1)S(1)}, u32[]{:S(2)}, u32[]{:S(2)}) %collective-permute-start) | collective-permute-done | bytes 65568 | tf_op jit(solution)/shard_map/ppermute | solution.py:334
  16.5 2.4 %all-to-all-done.got_ref = bf16[4,272,256]{2,1,0:T(8,128)(2,1)S(1)} async-done(((bf16[4,272,256]{2,1,0:T(8,128)(2,1)}), bf16[4,272,256]{2,1,0:T(8,128)(2,1)S(1)}, u32[]{:S(2)}, u32[]{:S(2)}) %all-to-all-start) | async-done | bytes 557088 | tf_op jit(solution)/shard_map/all_to_all | solution.py:330
  18.9 0.1 shard_map.124.group_ref
  19.0 3.8 %collective-permute-start.1 = (bf16[384,256]{1,0:T(8,128)(2,1)S(1)}, bf16[384,256]{1,0:T(8,128)(2,1)S(1)}, u32[]{:S(2)}, u32[]{:S(2)}) collective-permute-start(bf16[384,256]{1,0:T(8,128)(2,1)S(1)} %shard_map.124.group_ref), channel_id=1, source_target_pairs={{0,32},{32,64},{64,96},{96,128},{128,160},{160,192},{192,224},{224... | collective-permute-start | bytes 589832 | tf_op jit(solution)/shard_map/ppermute | solution.py:354
  22.8 2.5 %collective-permute-start.2 = (bf16[256,256]{1,0:T(8,128)(2,1)S(1)}, bf16[256,256]{1,0:T(8,128)(2,1)S(1)}, u32[]{:S(2)}, u32[]{:S(2)}) collective-permute-start(bf16[256,256]{1,0:T(8,128)(2,1)S(1)} %shard_map.127), channel_id=1, source_target_pairs={{0,8},{8,16},{16,24},{24,32},{32,40},{40,48},{48,56},{56,64},{64,7... | collective-permute-start | bytes 393224 | tf_op jit(solution)/shard_map/ppermute | solution.py:334
  25.3 0.1 shard_map.125
  25.4 1.1 %collective-permute-done.1.before_ref.kv4_ref = bf16[384,256]{1,0:T(8,128)(2,1)S(1)} collective-permute-done((bf16[384,256]{1,0:T(8,128)(2,1)S(1)}, bf16[384,256]{1,0:T(8,128)(2,1)S(1)}, u32[]{:S(2)}, u32[]{:S(2)}) %collective-permute-start.1) | collective-permute-done | bytes 196640 | tf_op jit(solution)/shard_map/ppermute | solution.py:354
  26.5 0.8 %shard_map.126 = bf16[4,256,256]{2,1,0:T(8,128)(2,1)} custom-call(f32[3,256,256]{2,1,0:T(8,128)S(1)} %get-tuple-element.12.part_ref, f32[3,8,256]{2,1,0:T(8,128)S(1)} %get-tuple-element.13.factor_ref, bf16[384,256]{1,0:T(8,128)(2,1)S(1)} %collective-permute-done.1.before_ref.kv4_ref), custom_call_target="tpu_custom_call" | custom-call | flops 1000000 | bytes 1000000 | tf_op jit(solution)/shard_map/pallas_call | solution.py:365
  27.4 0.0 copy-start.8
  27.4 5.5 %all-to-all-start.1 = ((bf16[4,256,256]{2,1,0:T(8,128)(2,1)}), bf16[4,256,256]{2,1,0:T(8,128)(2,1)S(1)}, u32[]{:S(2)}, u32[]{:S(2)}) async-start(bf16[4,256,256]{2,1,0:T(8,128)(2,1)} %shard_map.126), calls=%async_computation.1 | async-start | bytes 1048576 | tf_op jit(solution)/shard_map/all_to_all | solution.py:377
  32.9 0.0 collective-permute-done.2.pair_ref
  33.0 3.2 %shard_map.128.att_ref = bf16[128,1024]{1,0:T(8,128)(2,1)S(1)} custom-call(s32[1]{0:T(128)} %bitcast.begin_ref, s32[32]{0:T(128)S(1)} %copy-done.6, bf16[128,1024]{1,0:T(8,128)(2,1)S(1)} %copy-done.8, bf16[128,256]{1,0:T(8,128)(2,1)S(1)} %copy-done.1, bf16[128,256]{1,0:T(8,128)(2,1)S(1)} %collective-permute-done.near_ref.kv2_ref, ...), custom_call_target="tpu_custom_call" | custom-call | flops 10000000000 | bytes 100000000 | tf_op jit(solution)/shard_map/pallas_call | solution.py:378
  36.2 4.9 %all-to-all-done.1.carried_ref = bf16[4,256,256]{2,1,0:T(8,128)(2,1)S(1)} async-done(((bf16[4,256,256]{2,1,0:T(8,128)(2,1)}), bf16[4,256,256]{2,1,0:T(8,128)(2,1)S(1)}, u32[]{:S(2)}, u32[]{:S(2)}) %all-to-all-start.1) | async-done | bytes 524320 | tf_op jit(solution)/shard_map/all_to_all | solution.py:377
  41.0 0.3 shard_map.129
  41.4 14.7 %all_to_all.15.got_ref = bf16[8,16,2048]{2,1,0:T(8,128)(2,1)S(1)} all-to-all(bf16[8,16,2048]{2,1,0:T(8,128)(2,1)S(1)} %bitcast.4), channel_id=1, replica_groups=mesh['z'=16,'x'=4,'tp'=8] {'tp'}, dimensions={0} | all-to-all | bytes 1048576 | tf_op jit(solution)/shard_map/all_to_all | solution.py:395
  56.0 0.8 %shard_map.130 = (bf16[16,8192]{1,0:T(8,128)(2,1)}, bf16[16,8192]{1,0:T(8,128)(2,1)}) custom-call(bf16[8,16,2048]{2,1,0:T(8,128)(2,1)S(1)} %all_to_all.15.got_ref), custom_call_target="tpu_custom_call" | custom-call | bytes 1000000 | tf_op jit(solution)/shard_map/pallas_call | solution.py:396
  (8 shorter events, 0.0 us)
Async XLA Ops:
  3.1 4.5 %copy-start.1 = (bf16[128,256]{1,0:T(8,128)(2,1)S(1)}, bf16[128,256]{1,0:T(8,128)(2,1)}, u32[]{:S(2)}) copy-start(bf16[128,256]{1,0:T(8,128)(2,1)} %get-tuple-element.10.kv_ref.kv0_ref) | copy-start | bytes 196612
  3.1 10.1 %copy-start = (bf16[128,1024]{1,0:T(8,128)(2,1)S(1)}, bf16[128,1024]{1,0:T(8,128)(2,1)}, u32[]{:S(2)}) copy-start(bf16[128,1024]{1,0:T(8,128)(2,1)} %x_ref.1) | copy-start | bytes 786436
  3.1 10.1 %copy-start.2 = (bf16[128,256]{1,0:T(8,128)(2,1)S(1)}, bf16[128,256]{1,0:T(8,128)(2,1)}, u32[]{:S(2)}) copy-start(bf16[128,256]{1,0:T(8,128)(2,1)} %b_ref.1) | copy-start | bytes 196612
  3.2 10.1 %copy-start.3 = (bf16[128,256]{1,0:T(8,128)(2,1)S(1)}, bf16[128,256]{1,0:T(8,128)(2,1)}, u32[]{:S(2)}) copy-start(bf16[128,256]{1,0:T(8,128)(2,1)} %c_ref.3) | copy-start | bytes 196612
  3.2 10.1 %copy-start.4 = (f32[128,16]{0,1:T(8,128)S(1)}, f32[128,16]{0,1:T(8,128)}, u32[]{:S(2)}) copy-start(f32[128,16]{0,1:T(8,128)} %param.16) | copy-start | bytes 24580
  3.2 10.1 %copy-start.7 = (bf16[128,1024]{1,0:T(8,128)(2,1)S(1)}, bf16[128,1024]{1,0:T(8,128)(2,1)}, u32[]{:S(2)}) copy-start(bf16[128,1024]{1,0:T(8,128)(2,1)} %gate_ref.1) | copy-start | bytes 786436
  3.2 10.1 %copy-start.9 = (f32[1024]{0:T(1024)S(1)}, f32[1024]{0:T(1024)}, u32[]{:S(2)}) copy-start(f32[1024]{0:T(1024)} %param.18) | copy-start | bytes 12292
  3.2 15.7 %all-to-all-start = ((bf16[4,272,256]{2,1,0:T(8,128)(2,1)}), bf16[4,272,256]{2,1,0:T(8,128)(2,1)S(1)}, u32[]{:S(2)}, u32[]{:S(2)}) async-start(bf16[4,272,256]{2,1,0:T(8,128)(2,1)} %get-tuple-element.9), calls=%async_computation | async-start | bytes 1114112 | tf_op jit(solution)/shard_map/all_to_all | solution.py:330
  7.6 5.6 %copy-start.5 = (f32[16]{0:T(128)S(1)}, f32[16]{0:T(128)}, u32[]{:S(2)}) copy-start(f32[16]{0:T(128)} %rate_ref.1) | copy-start | bytes 196
  7.7 5.6 %copy-start.6 = (s32[32]{0:T(128)S(1)}, s32[32]{0:T(128)}, u32[]{:S(2)}) copy-start(s32[32]{0:T(128)} %doc_ref.3) | copy-start | bytes 388
  7.7 8.9 %collective-permute-start = (bf16[128,256]{1,0:T(8,128)(2,1)S(1)}, bf16[128,256]{1,0:T(8,128)(2,1)S(1)}, u32[]{:S(2)}, u32[]{:S(2)}) collective-permute-start(bf16[128,256]{1,0:T(8,128)(2,1)S(1)} %copy-done.1), channel_id=1, source_target_pairs={{0,16},{8,24},{16,32},{24,40},{32,48},{40,56},{48,64},{56,72},{64,... | collective-permute-start | bytes 196616 | tf_op jit(solution)/shard_map/ppermute | solution.py:334
  19.0 7.6 %collective-permute-start.1 = (bf16[384,256]{1,0:T(8,128)(2,1)S(1)}, bf16[384,256]{1,0:T(8,128)(2,1)S(1)}, u32[]{:S(2)}, u32[]{:S(2)}) collective-permute-start(bf16[384,256]{1,0:T(8,128)(2,1)S(1)} %shard_map.124.group_ref), channel_id=1, source_target_pairs={{0,32},{32,64},{64,96},{96,128},{128,160},{160,192},{192,224},{224... | collective-permute-start | bytes 589832 | tf_op jit(solution)/shard_map/ppermute | solution.py:354
  22.8 10.1 %collective-permute-start.2 = (bf16[256,256]{1,0:T(8,128)(2,1)S(1)}, bf16[256,256]{1,0:T(8,128)(2,1)S(1)}, u32[]{:S(2)}, u32[]{:S(2)}) collective-permute-start(bf16[256,256]{1,0:T(8,128)(2,1)S(1)} %shard_map.127), channel_id=1, source_target_pairs={{0,8},{8,16},{16,24},{24,32},{32,40},{40,48},{48,56},{56,64},{64,7... | collective-permute-start | bytes 393224 | tf_op jit(solution)/shard_map/ppermute | solution.py:334
  27.4 5.5 %copy-start.8 = (bf16[128,1024]{1,0:T(8,128)(2,1)S(1)}, bf16[128,1024]{1,0:T(8,128)(2,1)}, u32[]{:S(2)}) copy-start(bf16[128,1024]{1,0:T(8,128)(2,1)} %q_ref.1) | copy-start | bytes 786436
  27.4 13.6 %all-to-all-start.1 = ((bf16[4,256,256]{2,1,0:T(8,128)(2,1)}), bf16[4,256,256]{2,1,0:T(8,128)(2,1)S(1)}, u32[]{:S(2)}, u32[]{:S(2)}) async-start(bf16[4,256,256]{2,1,0:T(8,128)(2,1)} %shard_map.126), calls=%async_computation.1 | async-start | bytes 1048576 | tf_op jit(solution)/shard_map/all_to_all | solution.py:377
